TPU v7x, 512 devices: a whole 4x8x8 slice. The times are simulated.
512 devices in a mesh: member: 16 (over y, z_hi), space: 32 (over z_lo, x, core).
Axes of the slice: x: 4, y: 8, z: 8 (z_hi: 2, z_lo: 4; z = z_hi * 4 + z_lo), core: 2. Of those that a mesh axis runs over, the one named last changes fastest.
Arguments:
- ensemble: float32 [16, 26, 131072], P('member', None, 'space'), may hold values from -3 to 3, as said below
- target: float32 [26, 131072], P(None, 'space'), may hold values from -3 to 3, as said below
- chan_weight: float32 [26], replicated, may hold values from 0.2 to 2
- lat_band: int32 [1024], P('space'), may hold values from 0 to 359, as said below
Outputs:
- loss: float32 [], replicated
- grad_scaled: float32 [16, 26, 131072], P('member', None, 'space')
Inputs may be any that keep to these rules, and one draw needn't show every extreme that they name: `lat_band`: latitude row, counted from the south pole, of each block of 128 grid points; rows lie in the southern half. `ensemble`: multiples of 1/64. `target`: multiples of 1/64.
All inputs are finite; a program needn't handle non-finite values.
Results may differ from a plain program's by a relative error of at most 0.0003.
Values sent between devices are 32-bit elements; how exact they have to be, the bound alone decides.
A program may use at most 64 MiB of HBM per device.

v0:
```python
import math

import jax
import jax.numpy as jnp
from jax import lax
from jax.sharding import PartitionSpec as P

BLOCK = 128
BANDS = 720


def pair_sums(mine, others):

    def step(index, carry):
        spread, signs = carry
        other = lax.dynamic_index_in_dim(others, index, 0, keepdims=True)
        diff = mine - other
        return (spread + jnp.abs(diff), signs + jnp.sign(diff))

    zeros = jnp.zeros_like(mine)
    return lax.fori_loop(0, others.shape[0], step, (zeros, zeros))


def local(ensemble, target, chan_weight, lat_band):
    count = float(ensemble.shape[0] * lax.axis_size("member"))
    latitude = ((lat_band.astype(jnp.float32) + 0.5) / BANDS - 0.5) * math.pi
    block_area = jnp.cos(latitude)
    area = jnp.broadcast_to(block_area[:, None], (block_area.shape[0], BLOCK)).reshape(-1)
    local_area = jnp.sum(area)
    weights = area[None, :] * chan_weight[:, None]
    spread, signs = pair_sums(ensemble, lax.all_gather(ensemble, "member", axis=0, tiled=True))
    spread_term = jnp.sum(weights * jnp.sum(spread, axis=0))
    skill = ensemble - target[None]
    skill_term = jnp.sum(weights * jnp.sum(jnp.abs(skill), axis=0))
    local_loss = skill_term / count - spread_term / (2.0 * count * (count - 1.0))
    area_total = lax.psum(local_area, "space")
    loss_total = lax.psum(local_loss, ("member", "space"))
    channels = ensemble.shape[1]
    points = ensemble.shape[2] * lax.axis_size("space")
    loss = loss_total / (area_total * channels)
    scale = points * weights / area_total
    grad_scaled = scale[None] * (jnp.sign(skill) / count - signs / (count * (count - 1.0)))
    return (loss, grad_scaled)


def solution(mesh):
    in_specs = (P("member", None, "space"), P(None, "space"), P(), P("space"))
    out_specs = (P(), P("member", None, "space"))
    return jax.shard_map(local, mesh=mesh, in_specs=in_specs, out_specs=out_specs, check_vma=False)
```

profile of v0, /device:TPU:1, one launch (start us, length us, event | category | flops | bytes accessed | tf_op | source)
XLA Modules:
  0.0 348.8 jit_solution(10510126145452522147)
XLA Ops:
  7.2 0.0 all-gather.2.cloned.1.call-start
  7.2 2.1 copy.12
  9.3 0.0 copy-start
  9.3 0.0 copy-start.1
  9.3 0.0 copy-start.2
  9.3 0.0 all-gather.2.cloned.1.call-update
  9.4 0.8 multiply_cosine_fusion
  10.1 0.7 broadcast_reduce_fusion
  10.8 75.3 %psum.15 = f32[]{:T(128)} all-reduce(f32[]{:T(128)} %get-tuple-element.148), channel_id=1, replica_groups=mesh['member'=16,'space'=32] {'space'}, use_global_device_ids=true, to_apply=%region_6.7 | all-reduce | flops 1 | bytes 8 | tf_op jit(solution)/shard_map/psum | solution.py:36
  86.1 126.5 %all-gather.2.cloned.1.call-done = f32[16,26,4096]{2,1,0:T(8,128)} async-done(((f32[1,26,4096]{2,1,0:T(8,128)}), f32[16,26,4096]{2,1,0:T(8,128)}) %all-gather.2.cloned.1.call-update) | async-done | bytes 6815760 | tf_op jit(solution)/shard_map/all_gather | solution.py:31
  212.6 25.2 %while.16 = (s32[]{:T(128)}, f32[1,26,4096]{2,1,0:T(8,128)S(1)}, f32[1,26,4096]{2,1,0:T(8,128)S(1)}, f32[16,26,4096]{2,1,0:T(8,128)}, f32[1,26,4096]{2,1,0:T(8,128)}, /*index=5*/s32[]{:T(128)}, s32[]{:T(128)}) while((s32[]{:T(128)}, f32[1,26,4096]{2,1,0:T(8,128)S(1)}, f32[1,26,4096]{2,1,0:T(8,128)S(1)}, f32[16,26,4096]{2,1,0:T(8,128)}, ...), condition=%wide.region_2.3_spmd.clone, body=%wide.region_1.2_spmd.clone.sunk | while | flops 745475 | bytes 2555995 | solution.py:21
  212.6 1.6 select_add_fusion.3
  214.2 1.6 select_add_fusion.3
  215.7 1.6 select_add_fusion.3
  217.3 1.6 select_add_fusion.3
  218.9 1.6 select_add_fusion.3
  220.5 1.6 select_add_fusion.3
  222.1 1.6 select_add_fusion.3
  223.6 1.6 select_add_fusion.3
  225.2 1.6 select_add_fusion.3
  226.8 1.6 select_add_fusion.3
  228.4 1.6 select_add_fusion.3
  229.9 1.6 select_add_fusion.3
  231.5 1.6 select_add_fusion.3
  233.1 1.6 select_add_fusion.3
  234.7 1.6 select_add_fusion.3
  236.3 1.6 select_add_fusion.3
  237.8 0.0 copy-done
  237.8 0.0 copy-done.1
  237.8 0.0 copy-done.2
  237.9 3.2 divide_multiply_fusion
  241.0 1.1 fusion.1
  244.1 96.1 %psum.14 = f32[]{:T(128)} all-reduce(f32[]{:T(128)S(6)} %sub.21), channel_id=1, replica_groups=mesh['member'=16,'space'=32] {'member','space'}, use_global_device_ids=true, to_apply=%region_4.5 | all-reduce | flops 1 | bytes 8 | tf_op jit(solution)/shard_map/psum | solution.py:37
  (2 shorter events, 0.0 us)
Async XLA Ops:
  7.2 205.4 %all-gather.2.cloned.1.call-start = ((), (), s32[]{:S(2)}) async-start(), calls=%async_computation | async-start | bytes 8912896 | tf_op jit(solution)/shard_map/all_gather | solution.py:31
  9.3 228.5 %copy-start = (f32[1,26,4096]{2,0,1:T(1,128)S(1)}, f32[1,26,4096]{2,0,1:T(1,128)}, u32[]{:S(2)}) copy-start(f32[1,26,4096]{2,0,1:T(1,128)} %param.6) | copy-start | bytes 1277956
  9.3 228.5 %copy-start.1 = (f32[26,4096]{1,0:T(8,128)S(1)}, f32[26,4096]{1,0:T(8,128)}, u32[]{:S(2)}) copy-start(f32[26,4096]{1,0:T(8,128)} %param.7) | copy-start | bytes 1277956
  9.3 228.5 %copy-start.2 = (f32[26]{0:T(128)S(1)}, f32[26]{0:T(128)}, u32[]{:S(2)}) copy-start(f32[26]{0:T(128)} %param.8) | copy-start | bytes 316
Sparse Core Ops, SparseCore 0:
  11.2 201.3 all-gather.1
where the time goes:
time: 349 us
  blocking collectives  171 us (49%)
  waiting for transfers between devices  126 us (36%)
  other arithmetic  30.7 us (9%)
  between operations  17.8 us (5%)
    all_gather x1, waiting for transfers between devices, local(): lax.all_gather(ensemble, 'member', axis=0, tiled=True)  126 us
    psum x1, blocking collectives, local(): loss_total = lax.psum(local_loss, ('member', 'space'))  96.1 us
    psum x1, blocking collectives, local(): area_total = lax.psum(local_area, 'space')  75.3 us
    add x16, other arithmetic, step(): return (spread + jnp.abs(diff), signs + jnp.sign(diff))  24.9 us
  transfers between devices with their start and end apart: 1, of which 1 were waited for; matrix products, arithmetic and copies ran while one was open for 0% of the time, Pallas kernels for 0%

commit v1 on v0

v1 whole, which is shorter than its diff:
```python
import math

import jax
import jax.numpy as jnp
from jax import lax
from jax.experimental import pallas as pl
from jax.experimental.pallas import tpu as pltpu
from jax.sharding import PartitionSpec as P

BLOCK = 128
BANDS = 720
MESH = pl.DeviceIdType.MESH
ROWS = 4
NEAR = 8
PLANES = 2
CHUNKS = ((0, 6), (6, 7))


def kernel(
    members,
    spaces,
    ens,
    tgt,
    cw_hbm,
    lat_hbm,
    grad,
    loss,
    cw,
    lat,
    own,
    tgt_rows,
    sgn,
    scl,
    gat,
    sums,
    back,
    area,
    met_area,
    box_row,
    box_a1,
    box_a2,
    box_l1,
    box_l2,
    box_l3,
    local_sem,
    row_sem,
    send1,
    recv1,
    send2,
    recv2,
    send_a1,
    recv_a1,
    send_a2,
    recv_a2,
    send_l1,
    recv_l1,
    send_l2,
    recv_l2,
    send_l3,
    recv_l3,
):
    m = lax.axis_index("member")
    s = lax.axis_index("space")
    far = spaces // NEAR
    ny = members // PLANES
    nz = far * PLANES
    near_at = lax.rem(s, NEAR)
    far_at = lax.div(s, NEAR)
    y = lax.div(m, PLANES)
    z = lax.rem(m, PLANES) * far + far_at
    units = ens.shape[0]
    per = units // members
    channels = tgt.shape[0]
    groups = units // channels
    blocks = groups * ROWS

    def member_of(yy, zz):
        return lax.rem(yy + ny, ny) * PLANES + lax.div(lax.rem(zz + nz, nz), far)

    def place(yy, zz):
        return (member_of(yy, zz), lax.rem(lax.rem(zz + nz, nz), far) * NEAR + near_at)

    def near_peer(k):
        return (m, s - near_at + lax.rem(near_at + k, NEAR))

    def far_peer(k):
        return (m, lax.rem(far_at + k, far) * NEAR + near_at)

    def z_peer(k):
        return place(y, z + k)

    def y_peer(k):
        return place(y + k, z)

    own_copy = pltpu.make_async_copy(ens, own, local_sem.at[0])
    tgt_copy = pltpu.make_async_copy(tgt, tgt_rows, local_sem.at[1])
    cw_copy = pltpu.make_async_copy(cw_hbm, cw, local_sem.at[2])
    lat_copy = pltpu.make_async_copy(lat_hbm, lat, local_sem.at[3])
    lat_copy.start()
    cw_copy.start()
    own_copy.start()
    tgt_copy.start()

    quarter = nz // 4

    def met(n):
        step = lax.div(lax.div(n, 2) + 1, 2)
        dy = ny // 2 + step * (2 * lax.rem(lax.div(n, 2), 2) - 1)
        return place(y + dy, z + quarter * (1 - 2 * lax.rem(n, 2)))

    barrier = pltpu.get_barrier_semaphore()

    def greet(peer):
        pl.semaphore_signal(barrier, inc=1, device_id=peer, device_id_type=MESH)

    def greet_all(peer, start, count):
        def one(k, carry):
            greet(peer(k))
            return carry

        lax.fori_loop(start, count, one, 0)

    greet_all(met, 0, members)
    greet_all(near_peer, 1, NEAR)
    greet_all(z_peer, 1, nz)
    greet_all(y_peer, 1, ny)
    pl.semaphore_wait(barrier, members + (NEAR - 1) + (nz - 1) + (ny - 1))

    def push(src, dst, send, recv, device):
        pltpu.make_async_remote_copy(
            src_ref=src,
            dst_ref=dst,
            send_sem=send,
            recv_sem=recv,
            device_id=device,
            device_id_type=MESH,
        ).start()

    def exchange(source, landing, send, recv, chunk):
        def one(n, carry):
            device = met(n)
            j = device[0]
            push(source(j), landing(m), send.at[chunk, j], recv.at[chunk, m], device)
            return carry

        lax.fori_loop(0, members, one, 0)

    def arrived(ref, sem):
        pltpu.make_async_copy(ref, ref, sem).wait()

    def share(box, at, send, recv, peer, count):
        def one(k, carry):
            push(box.at[at], box.at[at], send.at[k], recv.at[at], peer(k))
            return carry

        lax.fori_loop(1, count, one, 0)

    def collect(box, at, send, recv, count):
        def one(k, carry):
            j = lax.rem(at + k, count)
            pltpu.make_async_copy(box.at[j], box.at[j], recv.at[j]).wait()
            pltpu.make_async_copy(box.at[at], box.at[at], send.at[k]).wait()
            return carry

        lax.fori_loop(1, count, one, 0)
        total = box[0]
        for j in range(1, count):
            total = total + box[j]
        return total

    for chunk, (first, size) in enumerate(CHUNKS):
        exchange(
            lambda j: ens.at[pl.ds(j * per + first, size)],
            lambda i: gat.at[i, pl.ds(first, size)],
            send1,
            recv1,
            chunk,
        )

    def along_rows(row):
        square = jnp.broadcast_to(row, (blocks, blocks))
        diagonal = lax.broadcasted_iota(jnp.int32, (blocks, blocks), 0) == lax.broadcasted_iota(
            jnp.int32, (blocks, blocks), 1
        )
        column = jnp.sum(jnp.where(diagonal, square, 0.0), axis=1, keepdims=True)
        return jnp.broadcast_to(column, (blocks, BLOCK))

    lat_copy.wait()
    latitude = ((lat[...].astype(jnp.float32) + 0.5) / BANDS - 0.5) * math.pi
    block_area = jnp.cos(latitude)
    box_row[0] = block_area
    push(box_row.at[0], box_row.at[1], row_sem.at[0], row_sem.at[1], place(y, z + quarter))
    wide = along_rows(block_area)
    for g in range(groups):
        area[g] = wide[g * ROWS : (g + 1) * ROWS]
    box_a1[near_at] = jnp.sum(wide, axis=0, keepdims=True)
    share(box_a1, near_at, send_a1, recv_a1, near_peer, NEAR)

    cw_copy.wait()
    own_copy.wait()
    tgt_copy.wait()

    def skill_rows(first, rows, acc):
        for g in range(groups):
            tiles = [
                tgt_rows[pl.ds(first, rows), pl.ds((g * ROWS + i) * BLOCK, BLOCK)] for i in range(ROWS)
            ]
            part = jnp.zeros((ROWS, BLOCK), jnp.float32)
            for r in range(rows):
                u = (first + r) * groups + g
                skill = own[u] - jnp.concatenate([tile[r : r + 1] for tile in tiles], axis=0)
                sgn[u] = jnp.clip(skill * 64.0, -1.0, 1.0) * 0.0625
                part = part + cw[first + r] * jnp.abs(skill)
            acc = acc + area[g] * part
        return acc

    def skill_octet(k, acc):
        return skill_rows(pl.multiple_of(k * 8, 8), 8, acc)

    octets = channels // 8
    skill_sum = lax.fori_loop(0, octets, skill_octet, jnp.zeros((ROWS, BLOCK), jnp.float32))
    if channels % 8:
        skill_sum = skill_rows(octets * 8, channels % 8, skill_sum)

    arrived(box_row.at[1], row_sem.at[1])
    met_wide = along_rows(box_row[1])
    for g in range(groups):
        met_area[g] = met_wide[g * ROWS : (g + 1) * ROWS]
    count = float(members)

    def pairs(places, acc):
        values = [
            jnp.concatenate([gat[j, i] for i in places], axis=0) * 64.0 for j in range(members)
        ]
        signs = [jnp.zeros_like(values[0]) for j in range(members)]
        for a in range(members):
            for b in range(a + 1, members):
                d = jnp.clip(values[a] - values[b], -1.0, 1.0)
                signs[a] = signs[a] + d
                signs[b] = signs[b] - d
        dot = values[0] * signs[0]
        for j in range(1, members):
            dot = dot + values[j] * signs[j]
        for n, i in enumerate(places):
            part = slice(n * ROWS, (n + 1) * ROWS)
            for j in range(members):
                sums[j, i] = signs[j][part]
            u = m * per + i
            acc = acc + (met_area[lax.rem(u, groups)] * cw[lax.div(u, groups)]) * dot[part]
        return acc

    spread_sum = jnp.zeros((ROWS, BLOCK), jnp.float32)
    for chunk, (first, size) in enumerate(CHUNKS):

        def wait_chunk(j, carry):
            arrived(gat.at[j, pl.ds(first, size)], recv1.at[chunk, j])
            return carry

        lax.fori_loop(0, members, wait_chunk, 0)
        spread_sum = lax.fori_loop(
            0,
            size // 2,
            lambda k, acc: pairs((first + 2 * k, first + 2 * k + 1), acc),
            spread_sum,
        )
        if size % 2:
            spread_sum = pairs((first + size - 1,), spread_sum)
        if first + size == per:
            mine = skill_sum * (1.0 / count) - spread_sum * (1.0 / (64.0 * count * (count - 1.0)))
            box_l1[near_at] = jnp.sum(mine, axis=0, keepdims=True)
            share(box_l1, near_at, send_l1, recv_l1, near_peer, NEAR)
        exchange(
            lambda j: sums.at[j, pl.ds(first, size)],
            lambda i: back.at[pl.ds(i * per + first, size)],
            send2,
            recv2,
            chunk,
        )

    area_near = collect(box_a1, near_at, send_a1, recv_a1, NEAR)
    box_a2[far_at] = area_near
    share(box_a2, far_at, send_a2, recv_a2, far_peer, far)
    loss_near = collect(box_l1, near_at, send_l1, recv_l1, NEAR)
    box_l2[z] = loss_near
    share(box_l2, z, send_l2, recv_l2, z_peer, nz)

    area_all = collect(box_a2, far_at, send_a2, recv_a2, far)
    area_total = jnp.sum(area_all, axis=1, keepdims=True)
    points = float(units * ROWS * BLOCK // channels * spaces)
    factor = jnp.broadcast_to(points / area_total, (ROWS, BLOCK))

    def scale_channel(c, carry):
        weight = cw[c]
        for g in range(groups):
            u = c * groups + g
            scale = area[g] * factor * weight
            sgn[u] = sgn[u] * scale
            scl[u] = scale * (1.0 / (count * (count - 1.0)))
        return carry

    lax.fori_loop(0, channels, scale_channel, 0)

    def finish(j, source, first, size):
        part = pl.ds(j * per + first, size)
        grad[part] = sgn[part] - scl[part] * source

    loss_z = collect(box_l2, z, send_l2, recv_l2, nz)
    box_l3[y] = loss_z
    share(box_l3, y, send_l3, recv_l3, y_peer, ny)

    for chunk, (first, size) in enumerate(CHUNKS):

        def take_back(n, carry):
            j = met(n)[0]
            part = back.at[pl.ds(j * per + first, size)]
            arrived(part, recv2.at[chunk, j])
            finish(j, part[...], first, size)
            return carry

        lax.fori_loop(0, members, take_back, 0)

    loss_all = collect(box_l3, y, send_l3, recv_l3, ny)
    loss_total = jnp.sum(loss_all, axis=1, keepdims=True)
    loss[...] = loss_total / (area_total * float(channels))

    for chunk, (first, size) in enumerate(CHUNKS):

        def wait_sent(j, carry):
            arrived(gat.at[j, pl.ds(first, size)], send1.at[chunk, j])
            arrived(sums.at[j, pl.ds(first, size)], send2.at[chunk, j])
            return carry

        lax.fori_loop(0, members, wait_sent, 0)
    arrived(box_row.at[0], row_sem.at[0])


def local(members, spaces, ensemble, target, chan_weight, lat_band):
    channels, points = target.shape
    units = channels * points // (ROWS * BLOCK)
    per = units // members
    far = spaces // NEAR
    ny = members // PLANES
    nz = far * PLANES
    f32 = jnp.float32
    dma = pltpu.SemaphoreType.DMA
    vmem = pl.BlockSpec(memory_space=pltpu.VMEM)
    hbm = pl.BlockSpec(memory_space=pltpu.HBM)
    whole = pltpu.VMEM((units, ROWS, BLOCK), f32)
    slabs = pltpu.VMEM((members, per, ROWS, BLOCK), f32)

    def box(n):
        return pltpu.VMEM((n, 1, BLOCK), f32)

    def in_hbm(x):
        return pltpu.with_memory_space_constraint(x, pltpu.HBM)

    def body(*refs):
        kernel(members, spaces, *refs)

    grad, loss = pl.pallas_call(
        body,
        out_shape=(
            jax.ShapeDtypeStruct((units, ROWS, BLOCK), f32),
            jax.ShapeDtypeStruct((1, 1), f32),
        ),
        in_specs=[hbm] * 4,
        out_specs=(vmem, vmem),
        scratch_shapes=[
            pltpu.SMEM(chan_weight.shape, f32),
            pltpu.VMEM((1, lat_band.shape[0]), lat_band.dtype),
            whole,
            pltpu.VMEM((channels, points), f32),
            whole,
            whole,
            slabs,
            slabs,
            whole,
            pltpu.VMEM((points // (ROWS * BLOCK), ROWS, BLOCK), f32),
            pltpu.VMEM((points // (ROWS * BLOCK), ROWS, BLOCK), f32),
            pltpu.VMEM((2, 1, lat_band.shape[0]), f32),
            box(NEAR),
            box(far),
            box(NEAR),
            box(nz),
            box(ny),
            dma((4,)),
            dma((2,)),
            dma((len(CHUNKS), members)),
            dma((len(CHUNKS), members)),
            dma((len(CHUNKS), members)),
            dma((len(CHUNKS), members)),
            dma((NEAR,)),
            dma((NEAR,)),
            dma((far,)),
            dma((far,)),
            dma((NEAR,)),
            dma((NEAR,)),
            dma((nz,)),
            dma((nz,)),
            dma((ny,)),
            dma((ny,)),
        ],
        compiler_params=pltpu.CompilerParams(
            collective_id=0, has_side_effects=True, vmem_limit_bytes=32 * 1024 * 1024
        ),
    )(
        in_hbm(ensemble.reshape(units, ROWS, BLOCK)),
        in_hbm(target),
        in_hbm(chan_weight),
        in_hbm(lat_band.reshape(1, -1)),
    )
    return loss.reshape(()), grad.reshape(1, channels, points)


def solution(mesh):
    members, spaces = mesh.shape["member"], mesh.shape["space"]

    def step(*args):
        return local(members, spaces, *args)

    in_specs = (P("member", None, "space"), P(None, "space"), P(), P("space"))
    out_specs = (P(), P("member", None, "space"))
    return jax.shard_map(step, mesh=mesh, in_specs=in_specs, out_specs=out_specs, check_vma=False)
```

time: 349 us -> 47.9 us (0.14)
  blocking collectives: 171 us -> 0 us
  waiting for transfers between devices: 126 us -> 0 us
  Pallas kernels: 0 us -> 44.3 us
  other arithmetic: 30.7 us -> 0 us
  between operations: 17.8 us -> 2.33 us
    psum x2 -> x0, blocking collectives: 171 us -> none  [the longest x1 96.1 us: local(): loss_total = lax.psum(local_loss, ('member', 'space'))]
    all_gather x1 -> x0, waiting for transfers between devices: 126 us -> none  [local(): lax.all_gather(ensemble, 'member', axis=0, tiled=True)]
    pallas_call x0 -> x1, Pallas kernels: none -> 44.3 us  [local(): pl.pallas_call(body, out_shape=(jax.ShapeDtypeStruct((units, ROWS, BLOCK)...]
    add x16 -> x0, other arithmetic: 24.9 us -> none  [step(): return (spread + jnp.abs(diff), signs + jnp.sign(diff))]
  transfers between devices with their start and end apart: 1 -> 0, of which waited for: 1 -> 0; matrix products, arithmetic and copies ran while one was open for 0% -> 0% of each run, Pallas kernels for 0% -> 0%
where the time goes in v1:
time: 47.9 us; the launch traced here: 47.3 us
  Pallas kernels  44.3 us (92%)
  between operations  2.33 us (5%)
  local copies, waits for them, and re-layouts  0.76 us (2%)
    pallas_call x1, Pallas kernels, local(): pl.pallas_call(body, out_shape=(jax.ShapeDtypeStruct((units, ROWS, BLOCK)...  44.3 us

profile of v1, /device:TPU:1, one launch (start us, length us, event | category | flops | bytes accessed | tf_op | source)
XLA Modules:
  0.0 47.3 jit_solution(15991526366862339521)
XLA Ops:
  0.6 44.3 %shard_map.59 = (f32[208,4,128]{2,1,0:T(4,128)S(1)}, f32[1,1]{1,0:T(1,128)}) custom-call(f32[208,4,128]{2,1,0:T(4,128)} %bitcast.5, f32[26,4096]{1,0:T(8,128)} %refs_1_.1, f32[26]{0:T(128)} %refs_2_.1, s32[1,32]{1,0:T(1,128)} %bitcast.6), custom_call_target="tpu_custom_call" | custom-call | tf_op jit(solution)/shard_map/pallas_call | solution.py:360
  45.5 0.8 %copy.11 = f32[1,26,4096]{2,0,1:T(1,128)} copy(f32[1,26,4096]{2,0,1:T(1,128)S(1)} %bitcast.4) | data formatting | bytes 851968

commit v2 on v1

--- a/solution.py
+++ b/solution.py
@@ -34,6 +34,8 @@
     gat,
     sums,
     back,
+    relay1,
+    relay2,
     area,
     met_area,
     box_row,
@@ -46,8 +48,12 @@
     row_sem,
     send1,
     recv1,
+    hop1,
+    fwd1,
     send2,
     recv2,
+    hop2,
+    fwd2,
     send_a1,
     recv_a1,
     send_a2,
@@ -136,14 +142,27 @@
             device_id_type=MESH,
         ).start()
 
-    def exchange(source, landing, send, recv, chunk):
+    twin = y + 1 - 2 * lax.rem(y, 2)
+    sides = (quarter, -quarter)
+
+    def exchange(source, landing, relay, send, recv, hop, chunk):
+        for side, dz in enumerate(sides):
+            j = member_of(y + ny // 2, z + dz)
+            push(source(j), relay.at[side], send.at[chunk, j], hop.at[chunk, side], place(twin, z + dz))
+
         def one(n, carry):
             device = met(n)
             j = device[0]
             push(source(j), landing(m), send.at[chunk, j], recv.at[chunk, m], device)
             return carry
 
-        lax.fori_loop(0, members, one, 0)
+        lax.fori_loop(PLANES, members, one, 0)
+
+    def forward(landing, relay, fwd, recv, hop, chunk):
+        for side, dz in enumerate(sides):
+            i = member_of(twin, z - dz)
+            arrived(relay.at[side], hop.at[chunk, side])
+            push(relay.at[side], landing(i), fwd.at[chunk, side], recv.at[chunk, i], place(twin + ny // 2, z))
 
     def arrived(ref, sem):
         pltpu.make_async_copy(ref, ref, sem).wait()
@@ -168,13 +187,21 @@
             total = total + box[j]
         return total
 
+    def gather(chunk):
+        first, size = CHUNKS[chunk]
+        part = pl.ds(first, size)
+        landing = lambda i: gat.at[i, part]
+        return landing, relay1.at[:, part]
+
+    def scatter(chunk):
+        first, size = CHUNKS[chunk]
+        landing = lambda i: back.at[pl.ds(i * per + first, size)]
+        return landing, relay2.at[:, pl.ds(first, size)]
+
     for chunk, (first, size) in enumerate(CHUNKS):
+        landing, relay = gather(chunk)
         exchange(
-            lambda j: ens.at[pl.ds(j * per + first, size)],
-            lambda i: gat.at[i, pl.ds(first, size)],
-            send1,
-            recv1,
-            chunk,
+            lambda j: ens.at[pl.ds(j * per + first, size)], landing, relay, send1, recv1, hop1, chunk
         )
 
     def along_rows(row):
@@ -195,6 +222,9 @@
         area[g] = wide[g * ROWS : (g + 1) * ROWS]
     box_a1[near_at] = jnp.sum(wide, axis=0, keepdims=True)
     share(box_a1, near_at, send_a1, recv_a1, near_peer, NEAR)
+
+    landing, relay = gather(0)
+    forward(landing, relay, fwd1, recv1, hop1, 0)
 
     cw_copy.wait()
     own_copy.wait()
@@ -221,6 +251,10 @@
     skill_sum = lax.fori_loop(0, octets, skill_octet, jnp.zeros((ROWS, BLOCK), jnp.float32))
     if channels % 8:
         skill_sum = skill_rows(octets * 8, channels % 8, skill_sum)
+
+    for chunk in range(1, len(CHUNKS)):
+        landing, relay = gather(chunk)
+        forward(landing, relay, fwd1, recv1, hop1, chunk)
 
     arrived(box_row.at[1], row_sem.at[1])
     met_wide = along_rows(box_row[1])
@@ -269,13 +303,11 @@
             mine = skill_sum * (1.0 / count) - spread_sum * (1.0 / (64.0 * count * (count - 1.0)))
             box_l1[near_at] = jnp.sum(mine, axis=0, keepdims=True)
             share(box_l1, near_at, send_l1, recv_l1, near_peer, NEAR)
-        exchange(
-            lambda j: sums.at[j, pl.ds(first, size)],
-            lambda i: back.at[pl.ds(i * per + first, size)],
-            send2,
-            recv2,
-            chunk,
-        )
+        landing, relay = scatter(chunk)
+        exchange(lambda j: sums.at[j, pl.ds(first, size)], landing, relay, send2, recv2, hop2, chunk)
+    for chunk in range(len(CHUNKS)):
+        landing, relay = scatter(chunk)
+        forward(landing, relay, fwd2, recv2, hop2, chunk)
 
     area_near = collect(box_a1, near_at, send_a1, recv_a1, NEAR)
     box_a2[far_at] = area_near
@@ -331,6 +363,9 @@
             return carry
 
         lax.fori_loop(0, members, wait_sent, 0)
+        for side in range(len(sides)):
+            arrived(relay1.at[side, pl.ds(first, size)], fwd1.at[chunk, side])
+            arrived(relay2.at[side, pl.ds(first, size)], fwd2.at[chunk, side])
     arrived(box_row.at[0], row_sem.at[0])
 
 
@@ -346,6 +381,7 @@
     vmem = pl.BlockSpec(memory_space=pltpu.VMEM)
     hbm = pl.BlockSpec(memory_space=pltpu.HBM)
     whole = pltpu.VMEM((units, ROWS, BLOCK), f32)
+    relay = pltpu.VMEM((PLANES, per, ROWS, BLOCK), f32)
     slabs = pltpu.VMEM((members, per, ROWS, BLOCK), f32)
 
     def box(n):
@@ -375,6 +411,8 @@
             slabs,
             slabs,
             whole,
+            relay,
+            relay,
             pltpu.VMEM((points // (ROWS * BLOCK), ROWS, BLOCK), f32),
             pltpu.VMEM((points // (ROWS * BLOCK), ROWS, BLOCK), f32),
             pltpu.VMEM((2, 1, lat_band.shape[0]), f32),
@@ -387,8 +425,12 @@
             dma((2,)),
             dma((len(CHUNKS), members)),
             dma((len(CHUNKS), members)),
+            dma((len(CHUNKS), PLANES)),
+            dma((len(CHUNKS), PLANES)),
             dma((len(CHUNKS), members)),
             dma((len(CHUNKS), members)),
+            dma((len(CHUNKS), PLANES)),
+            dma((len(CHUNKS), PLANES)),
             dma((NEAR,)),
             dma((NEAR,)),
             dma((far,)),

time: 47.9 us -> 50.9 us (1.063)
  the two profiles are of different devices: /device:TPU:1 before, /device:TPU:6 now
where the time goes in v2:
time: 50.9 us; the launch traced here: 50.8 us
  Pallas kernels  47.7 us (94%)
  between operations  2.33 us (5%)
  local copies, waits for them, and re-layouts  0.76 us (1%)
    pallas_call x1, Pallas kernels, local(): pl.pallas_call(body, out_shape=(jax.ShapeDtypeStruct((units, ROWS, BLOCK)...  47.7 us

profile of v2, /device:TPU:6, one launch (start us, length us, event | category | flops | bytes accessed | tf_op | source)
XLA Modules:
  0.0 50.8 jit_solution(13395811475918705714)
XLA Ops:
  0.6 47.7 %shard_map.59 = (f32[208,4,128]{2,1,0:T(4,128)S(1)}, f32[1,1]{1,0:T(1,128)}) custom-call(f32[208,4,128]{2,1,0:T(4,128)} %bitcast.5, f32[26,4096]{1,0:T(8,128)} %refs_1_.1, f32[26]{0:T(128)} %refs_2_.1, s32[1,32]{1,0:T(1,128)} %bitcast.6), custom_call_target="tpu_custom_call" | custom-call | tf_op jit(solution)/shard_map/pallas_call | solution.py:396
  48.9 0.8 %copy.11 = f32[1,26,4096]{2,0,1:T(1,128)} copy(f32[1,26,4096]{2,0,1:T(1,128)S(1)} %bitcast.4) | data formatting | bytes 851968

commit v3 on v1

--- a/solution.py
+++ b/solution.py
@@ -40,6 +40,7 @@
     box_a1,
     box_a2,
     box_l1,
+    box_near,
     box_l2,
     box_l3,
     local_sem,
@@ -74,23 +75,17 @@
     groups = units // channels
     blocks = groups * ROWS
 
-    def member_of(yy, zz):
-        return lax.rem(yy + ny, ny) * PLANES + lax.div(lax.rem(zz + nz, nz), far)
-
-    def place(yy, zz):
-        return (member_of(yy, zz), lax.rem(lax.rem(zz + nz, nz), far) * NEAR + near_at)
-
-    def near_peer(k):
-        return (m, s - near_at + lax.rem(near_at + k, NEAR))
-
-    def far_peer(k):
-        return (m, lax.rem(far_at + k, far) * NEAR + near_at)
-
-    def z_peer(k):
-        return place(y, z + k)
-
-    def y_peer(k):
-        return place(y + k, z)
+    y_at = [lax.rem(y + k, ny) for k in range(ny)]
+    z_at = [lax.rem(z + k, nz) for k in range(nz)]
+
+    def place(dy, dz):
+        zz = z_at[dz % nz]
+        return (y_at[dy % ny] * PLANES + lax.div(zz, far), lax.rem(zz, far) * NEAR + near_at)
+
+    near_base = s - near_at
+    near_peers = [(m, near_base + lax.rem(near_at + k, NEAR)) for k in range(1, NEAR)]
+    far_peers = [(m, lax.rem(far_at + k, far) * NEAR + near_at) for k in range(1, far)]
+    z_peers = [place(0, k) for k in range(1, nz)]
 
     own_copy = pltpu.make_async_copy(ens, own, local_sem.at[0])
     tgt_copy = pltpu.make_async_copy(tgt, tgt_rows, local_sem.at[1])
@@ -102,29 +97,16 @@
     tgt_copy.start()
 
     quarter = nz // 4
-
-    def met(n):
-        step = lax.div(lax.div(n, 2) + 1, 2)
-        dy = ny // 2 + step * (2 * lax.rem(lax.div(n, 2), 2) - 1)
-        return place(y + dy, z + quarter * (1 - 2 * lax.rem(n, 2)))
+    steps = sorted(range(ny), key=lambda k: -min(k, ny - k))
+    met = [place(dy, dz) for dy in steps for dz in (quarter, -quarter)]
+    upper = [place(dy, quarter) for dy in range(ny)]
 
     barrier = pltpu.get_barrier_semaphore()
-
-    def greet(peer):
+    fresh = [k for k in range(1, nz) if k not in (quarter, nz - quarter)]
+    greeted = met + near_peers + [place(0, k) for k in fresh]
+    for peer in greeted:
         pl.semaphore_signal(barrier, inc=1, device_id=peer, device_id_type=MESH)
-
-    def greet_all(peer, start, count):
-        def one(k, carry):
-            greet(peer(k))
-            return carry
-
-        lax.fori_loop(start, count, one, 0)
-
-    greet_all(met, 0, members)
-    greet_all(near_peer, 1, NEAR)
-    greet_all(z_peer, 1, nz)
-    greet_all(y_peer, 1, ny)
-    pl.semaphore_wait(barrier, members + (NEAR - 1) + (nz - 1) + (ny - 1))
+    pl.semaphore_wait(barrier, len(greeted))
 
     def push(src, dst, send, recv, device):
         pltpu.make_async_remote_copy(
@@ -136,30 +118,28 @@
             device_id_type=MESH,
         ).start()
 
-    def exchange(source, landing, send, recv, chunk):
-        def one(n, carry):
-            device = met(n)
+    def exchange(source, landing, send, recv, chunk, peers):
+        for device in peers:
             j = device[0]
             push(source(j), landing(m), send.at[chunk, j], recv.at[chunk, m], device)
-            return carry
-
-        lax.fori_loop(0, members, one, 0)
 
     def arrived(ref, sem):
         pltpu.make_async_copy(ref, ref, sem).wait()
 
-    def share(box, at, send, recv, peer, count):
-        def one(k, carry):
-            push(box.at[at], box.at[at], send.at[k], recv.at[at], peer(k))
-            return carry
-
-        lax.fori_loop(1, count, one, 0)
-
-    def collect(box, at, send, recv, count):
+    def share(box, at, send, recv, peers):
+        for k, peer in enumerate(peers):
+            push(box.at[at], box.at[at], send.at[k], recv.at[at], peer)
+
+    def sent(box, send, peers):
+        for k in range(len(peers)):
+            arrived(box.at[0], send.at[k])
+
+    def collect(box, at, recv):
+        count = box.shape[0]
+
         def one(k, carry):
             j = lax.rem(at + k, count)
-            pltpu.make_async_copy(box.at[j], box.at[j], recv.at[j]).wait()
-            pltpu.make_async_copy(box.at[at], box.at[at], send.at[k]).wait()
+            arrived(box.at[j], recv.at[j])
             return carry
 
         lax.fori_loop(1, count, one, 0)
@@ -175,6 +155,7 @@
             send1,
             recv1,
             chunk,
+            met,
         )
 
     def along_rows(row):
@@ -189,12 +170,12 @@
     latitude = ((lat[...].astype(jnp.float32) + 0.5) / BANDS - 0.5) * math.pi
     block_area = jnp.cos(latitude)
     box_row[0] = block_area
-    push(box_row.at[0], box_row.at[1], row_sem.at[0], row_sem.at[1], place(y, z + quarter))
+    push(box_row.at[0], box_row.at[1], row_sem.at[0], row_sem.at[1], place(0, quarter))
     wide = along_rows(block_area)
     for g in range(groups):
         area[g] = wide[g * ROWS : (g + 1) * ROWS]
     box_a1[near_at] = jnp.sum(wide, axis=0, keepdims=True)
-    share(box_a1, near_at, send_a1, recv_a1, near_peer, NEAR)
+    share(box_a1, near_at, send_a1, recv_a1, near_peers)
 
     cw_copy.wait()
     own_copy.wait()
@@ -257,6 +238,10 @@
             return carry
 
         lax.fori_loop(0, members, wait_chunk, 0)
+        if chunk == 0:
+            area_near = collect(box_a1, near_at, recv_a1)
+            box_a2[far_at] = area_near
+            share(box_a2, far_at, send_a2, recv_a2, far_peers)
         spread_sum = lax.fori_loop(
             0,
             size // 2,
@@ -265,26 +250,35 @@
         )
         if size % 2:
             spread_sum = pairs((first + size - 1,), spread_sum)
-        if first + size == per:
-            mine = skill_sum * (1.0 / count) - spread_sum * (1.0 / (64.0 * count * (count - 1.0)))
-            box_l1[near_at] = jnp.sum(mine, axis=0, keepdims=True)
-            share(box_l1, near_at, send_l1, recv_l1, near_peer, NEAR)
-        exchange(
-            lambda j: sums.at[j, pl.ds(first, size)],
-            lambda i: back.at[pl.ds(i * per + first, size)],
-            send2,
-            recv2,
-            chunk,
-        )
-
-    area_near = collect(box_a1, near_at, send_a1, recv_a1, NEAR)
-    box_a2[far_at] = area_near
-    share(box_a2, far_at, send_a2, recv_a2, far_peer, far)
-    loss_near = collect(box_l1, near_at, send_l1, recv_l1, NEAR)
-    box_l2[z] = loss_near
-    share(box_l2, z, send_l2, recv_l2, z_peer, nz)
-
-    area_all = collect(box_a2, far_at, send_a2, recv_a2, far)
+        def send_back(peers):
+            exchange(
+                lambda j: sums.at[j, pl.ds(first, size)],
+                lambda i: back.at[pl.ds(i * per + first, size)],
+                send2,
+                recv2,
+                chunk,
+                peers,
+            )
+
+        if first + size < per:
+            send_back(met)
+
+    mine = skill_sum * (1.0 / count) - spread_sum * (1.0 / (64.0 * count * (count - 1.0)))
+    box_l1[near_at] = jnp.sum(mine, axis=0, keepdims=True)
+    share(box_l1, near_at, send_l1, recv_l1, near_peers)
+    send_back(met[:5])
+    loss_near = collect(box_l1, near_at, recv_l1)
+    box_near[0] = loss_near
+    for k, peer in enumerate(upper):
+        push(box_near.at[0], box_l2.at[y], send_l2.at[k], recv_l2.at[y], peer)
+    send_back(met[5:10])
+    arrived(box_l2.at[y], recv_l2.at[y])
+    loss_y = collect(box_l2, y, recv_l2)
+    box_l3[z] = loss_y
+    share(box_l3, z, send_l3, recv_l3, z_peers)
+    send_back(met[10:])
+
+    area_all = collect(box_a2, far_at, recv_a2)
     area_total = jnp.sum(area_all, axis=1, keepdims=True)
     points = float(units * ROWS * BLOCK // channels * spaces)
     factor = jnp.broadcast_to(points / area_total, (ROWS, BLOCK))
@@ -304,14 +298,9 @@
         part = pl.ds(j * per + first, size)
         grad[part] = sgn[part] - scl[part] * source
 
-    loss_z = collect(box_l2, z, send_l2, recv_l2, nz)
-    box_l3[y] = loss_z
-    share(box_l3, y, send_l3, recv_l3, y_peer, ny)
-
     for chunk, (first, size) in enumerate(CHUNKS):
 
-        def take_back(n, carry):
-            j = met(n)[0]
+        def take_back(j, carry):
             part = back.at[pl.ds(j * per + first, size)]
             arrived(part, recv2.at[chunk, j])
             finish(j, part[...], first, size)
@@ -319,7 +308,7 @@
 
         lax.fori_loop(0, members, take_back, 0)
 
-    loss_all = collect(box_l3, y, send_l3, recv_l3, ny)
+    loss_all = collect(box_l3, z, recv_l3)
     loss_total = jnp.sum(loss_all, axis=1, keepdims=True)
     loss[...] = loss_total / (area_total * float(channels))
 
@@ -332,6 +321,11 @@
 
         lax.fori_loop(0, members, wait_sent, 0)
     arrived(box_row.at[0], row_sem.at[0])
+    sent(box_a1, send_a1, near_peers)
+    sent(box_a2, send_a2, far_peers)
+    sent(box_l1, send_l1, near_peers)
+    sent(box_l2, send_l2, upper)
+    sent(box_l3, send_l3, z_peers)
 
 
 def local(members, spaces, ensemble, target, chan_weight, lat_band):
@@ -381,8 +375,9 @@
             box(NEAR),
             box(far),
             box(NEAR),
+            box(1),
+            box(ny),
             box(nz),
-            box(ny),
             dma((4,)),
             dma((2,)),
             dma((len(CHUNKS), members)),
@@ -395,10 +390,10 @@
             dma((far,)),
             dma((NEAR,)),
             dma((NEAR,)),
+            dma((ny,)),
+            dma((ny,)),
             dma((nz,)),
             dma((nz,)),
-            dma((ny,)),
-            dma((ny,)),
         ],
         compiler_params=pltpu.CompilerParams(
             collective_id=0, has_side_effects=True, vmem_limit_bytes=32 * 1024 * 1024

time: 47.9 us -> 49.4 us (1.031)
  Pallas kernels: 44.3 us -> 45.8 us
    pallas_call x1, Pallas kernels: 44.3 us -> 45.8 us  [local(): pl.pallas_call(body, out_shape=(jax.ShapeDtypeStruct((units, ROWS, BLOCK)...]
where the time goes in v3:
time: 49.4 us; the launch traced here: 48.9 us
  Pallas kernels  45.8 us (93%)
  between operations  2.33 us (5%)
  local copies, waits for them, and re-layouts  0.76 us (2%)
    pallas_call x1, Pallas kernels, local(): pl.pallas_call(body, out_shape=(jax.ShapeDtypeStruct((units, ROWS, BLOCK)...  45.8 us

profile of v3, /device:TPU:1, one launch (start us, length us, event | category | flops | bytes accessed | tf_op | source)
XLA Modules:
  0.0 48.9 jit_solution(251288235939645227)
XLA Ops:
  0.6 45.8 %shard_map.59 = (f32[208,4,128]{2,1,0:T(4,128)S(1)}, f32[1,1]{1,0:T(1,128)}) custom-call(f32[208,4,128]{2,1,0:T(4,128)} %bitcast.5, f32[26,4096]{1,0:T(8,128)} %refs_1_.1, f32[26]{0:T(128)} %refs_2_.1, s32[1,32]{1,0:T(1,128)} %bitcast.6), custom_call_target="tpu_custom_call" | custom-call | tf_op jit(solution)/shard_map/pallas_call | solution.py:354
  47.0 0.8 %copy.11 = f32[1,26,4096]{2,0,1:T(1,128)} copy(f32[1,26,4096]{2,0,1:T(1,128)S(1)} %bitcast.4) | data formatting | bytes 851968

commit v4 on v1

--- a/solution.py
+++ b/solution.py
@@ -92,6 +92,29 @@
     def y_peer(k):
         return place(y + k, z)
 
+    quarter = nz // 4
+
+    def met(n):
+        step = lax.div(lax.div(n, 2) + 1, 2)
+        dy = ny // 2 + step * (2 * lax.rem(lax.div(n, 2), 2) - 1)
+        return place(y + dy, z + quarter * (1 - 2 * lax.rem(n, 2)))
+
+    barrier = pltpu.get_barrier_semaphore()
+
+    def greet(peer):
+        pl.semaphore_signal(barrier, inc=1, device_id=peer, device_id_type=MESH)
+
+    def greet_all(peer, start, count):
+        def one(k, carry):
+            greet(peer(k))
+            return carry
+
+        lax.fori_loop(start, count, one, 0)
+
+    greet_all(met, 0, members)
+    greet_all(near_peer, 1, NEAR)
+    greet_all(z_peer, 1, nz)
+    greet_all(y_peer, 1, ny)
     own_copy = pltpu.make_async_copy(ens, own, local_sem.at[0])
     tgt_copy = pltpu.make_async_copy(tgt, tgt_rows, local_sem.at[1])
     cw_copy = pltpu.make_async_copy(cw_hbm, cw, local_sem.at[2])
@@ -101,29 +124,6 @@
     own_copy.start()
     tgt_copy.start()
 
-    quarter = nz // 4
-
-    def met(n):
-        step = lax.div(lax.div(n, 2) + 1, 2)
-        dy = ny // 2 + step * (2 * lax.rem(lax.div(n, 2), 2) - 1)
-        return place(y + dy, z + quarter * (1 - 2 * lax.rem(n, 2)))
-
-    barrier = pltpu.get_barrier_semaphore()
-
-    def greet(peer):
-        pl.semaphore_signal(barrier, inc=1, device_id=peer, device_id_type=MESH)
-
-    def greet_all(peer, start, count):
-        def one(k, carry):
-            greet(peer(k))
-            return carry
-
-        lax.fori_loop(start, count, one, 0)
-
-    greet_all(met, 0, members)
-    greet_all(near_peer, 1, NEAR)
-    greet_all(z_peer, 1, nz)
-    greet_all(y_peer, 1, ny)
     pl.semaphore_wait(barrier, members + (NEAR - 1) + (nz - 1) + (ny - 1))
 
     def push(src, dst, send, recv, device):
@@ -257,6 +257,10 @@
             return carry
 
         lax.fori_loop(0, members, wait_chunk, 0)
+        if chunk == 0:
+            area_near = collect(box_a1, near_at, send_a1, recv_a1, NEAR)
+            box_a2[far_at] = area_near
+            share(box_a2, far_at, send_a2, recv_a2, far_peer, far)
         spread_sum = lax.fori_loop(
             0,
             size // 2,
@@ -277,12 +281,12 @@
             chunk,
         )
 
-    area_near = collect(box_a1, near_at, send_a1, recv_a1, NEAR)
-    box_a2[far_at] = area_near
-    share(box_a2, far_at, send_a2, recv_a2, far_peer, far)
     loss_near = collect(box_l1, near_at, send_l1, recv_l1, NEAR)
     box_l2[z] = loss_near
     share(box_l2, z, send_l2, recv_l2, z_peer, nz)
+    loss_z = collect(box_l2, z, send_l2, recv_l2, nz)
+    box_l3[y] = loss_z
+    share(box_l3, y, send_l3, recv_l3, y_peer, ny)
 
     area_all = collect(box_a2, far_at, send_a2, recv_a2, far)
     area_total = jnp.sum(area_all, axis=1, keepdims=True)
@@ -304,9 +308,6 @@
         part = pl.ds(j * per + first, size)
         grad[part] = sgn[part] - scl[part] * source
 
-    loss_z = collect(box_l2, z, send_l2, recv_l2, nz)
-    box_l3[y] = loss_z
-    share(box_l3, y, send_l3, recv_l3, y_peer, ny)
 
     for chunk, (first, size) in enumerate(CHUNKS):
 

time: 47.9 us -> 47.5 us (level)
  no operation moved by 1% of the time
where the time goes in v4:
time: 47.5 us; the launch traced here: 47.4 us
  Pallas kernels  44.3 us (93%)
  between operations  2.33 us (5%)
  local copies, waits for them, and re-layouts  0.76 us (2%)
    pallas_call x1, Pallas kernels, local(): pl.pallas_call(body, out_shape=(jax.ShapeDtypeStruct((units, ROWS, BLOCK)...  44.3 us

profile of v4, /device:TPU:1, one launch (start us, length us, event | category | flops | bytes accessed | tf_op | source)
XLA Modules:
  0.0 47.4 jit_solution(16464144038409224138)
XLA Ops:
  0.6 44.3 %shard_map.59 = (f32[208,4,128]{2,1,0:T(4,128)S(1)}, f32[1,1]{1,0:T(1,128)}) custom-call(f32[208,4,128]{2,1,0:T(4,128)} %bitcast.5, f32[26,4096]{1,0:T(8,128)} %refs_1_.1, f32[26]{0:T(128)} %refs_2_.1, s32[1,32]{1,0:T(1,128)} %bitcast.6), custom_call_target="tpu_custom_call" | custom-call | tf_op jit(solution)/shard_map/pallas_call | solution.py:361
  45.5 0.8 %copy.11 = f32[1,26,4096]{2,0,1:T(1,128)} copy(f32[1,26,4096]{2,0,1:T(1,128)S(1)} %bitcast.4) | data formatting | bytes 851968

commit v5 on v4

--- a/solution.py
+++ b/solution.py
@@ -23,8 +23,7 @@
     tgt,
     cw_hbm,
     lat_hbm,
-    grad,
-    loss,
+    result,
     cw,
     lat,
     own,
@@ -95,9 +94,10 @@
     quarter = nz // 4
 
     def met(n):
-        step = lax.div(lax.div(n, 2) + 1, 2)
-        dy = ny // 2 + step * (2 * lax.rem(lax.div(n, 2), 2) - 1)
-        return place(y + dy, z + quarter * (1 - 2 * lax.rem(n, 2)))
+        pair, turn = lax.div(n, 4), lax.rem(n, 4)
+        dy = ny // 2 - pair + lax.rem(turn, 2) * (2 * pair - ny + 1)
+        dz = quarter * (1 - 2 * lax.rem(lax.div(turn + 1, 2), 2))
+        return place(y + dy, z + dz)
 
     barrier = pltpu.get_barrier_semaphore()
 
@@ -306,7 +306,7 @@
 
     def finish(j, source, first, size):
         part = pl.ds(j * per + first, size)
-        grad[part] = sgn[part] - scl[part] * source
+        result[part] = sgn[part] - scl[part] * source
 
 
     for chunk, (first, size) in enumerate(CHUNKS):
@@ -322,7 +322,7 @@
 
     loss_all = collect(box_l3, y, send_l3, recv_l3, ny)
     loss_total = jnp.sum(loss_all, axis=1, keepdims=True)
-    loss[...] = loss_total / (area_total * float(channels))
+    result[units] = jnp.broadcast_to(loss_total / (area_total * float(channels)), (ROWS, BLOCK))
 
     for chunk, (first, size) in enumerate(CHUNKS):
 
@@ -333,6 +333,16 @@
 
         lax.fori_loop(0, members, wait_sent, 0)
     arrived(box_row.at[0], row_sem.at[0])
+
+
+def deliver(result, grad, loss, last, sem):
+    grad_copy = pltpu.make_async_copy(result.at[pl.ds(0, grad.shape[0])], grad, sem.at[0])
+    grad_copy.start()
+    last[...] = result[grad.shape[0], 0:1, 0:1]
+    loss_copy = pltpu.make_async_copy(last, loss, sem.at[1])
+    loss_copy.start()
+    loss_copy.wait()
+    grad_copy.wait()
 
 
 def local(members, spaces, ensemble, target, chan_weight, lat_band):
@@ -358,14 +368,11 @@
     def body(*refs):
         kernel(members, spaces, *refs)
 
-    grad, loss = pl.pallas_call(
+    result = pl.pallas_call(
         body,
-        out_shape=(
-            jax.ShapeDtypeStruct((units, ROWS, BLOCK), f32),
-            jax.ShapeDtypeStruct((1, 1), f32),
-        ),
+        out_shape=jax.ShapeDtypeStruct((units + 1, ROWS, BLOCK), f32),
         in_specs=[hbm] * 4,
-        out_specs=(vmem, vmem),
+        out_specs=vmem,
         scratch_shapes=[
             pltpu.SMEM(chan_weight.shape, f32),
             pltpu.VMEM((1, lat_band.shape[0]), lat_band.dtype),
@@ -410,6 +417,17 @@
         in_hbm(chan_weight),
         in_hbm(lat_band.reshape(1, -1)),
     )
+    grad, loss = pl.pallas_call(
+        deliver,
+        out_shape=(
+            jax.ShapeDtypeStruct((units, ROWS, BLOCK), f32),
+            jax.ShapeDtypeStruct((1, 1), f32),
+        ),
+        in_specs=[vmem],
+        out_specs=(hbm, hbm),
+        scratch_shapes=[pltpu.VMEM((1, 1), f32), dma((2,))],
+        compiler_params=pltpu.CompilerParams(vmem_limit_bytes=32 * 1024 * 1024),
+    )(result)
     return loss.reshape(()), grad.reshape(1, channels, points)
 
 

time: 47.5 us -> 45.4 us (0.956)
  between operations: 2.33 us -> 0.64 us
  local copies, waits for them, and re-layouts: 0.76 us -> 0 us
    unnamed x1 -> x0, local copies, waits for them, and re-layouts: 0.76 us -> none
    pallas_call x1 -> x2, Pallas kernels: 44.3 us -> 44.5 us  [the longest x1 43.7 us: local(): pl.pallas_call(body, out_shape=jax.ShapeDtypeStruct((units + 1, ROWS, BLO...]
where the time goes in v5:
time: 45.4 us; the launch traced here: 45.1 us
  Pallas kernels  44.5 us (98%)
  between operations  0.64 us (1%)
    pallas_call x1, Pallas kernels, local(): pl.pallas_call(body, out_shape=jax.ShapeDtypeStruct((units + 1, ROWS, BLO...  43.7 us

profile of v5, /device:TPU:1, one launch (start us, length us, event | category | flops | bytes accessed | tf_op | source)
XLA Modules:
  0.0 45.1 jit_solution(8503225683516790307)
XLA Ops:
  0.6 43.7 %shard_map.59.result = f32[209,4,128]{2,1,0:T(4,128)S(1)} custom-call(f32[208,4,128]{2,1,0:T(4,128)} %bitcast.4, f32[26,4096]{1,0:T(8,128)} %refs_1_.1, f32[26]{0:T(128)} %refs_2_.1, s32[1,32]{1,0:T(1,128)} %bitcast.5), custom_call_target="tpu_custom_call" | custom-call | tf_op jit(solution)/shard_map/pallas_call | solution.py:371
  44.4 0.8 %shard_map.60 = (f32[208,4,128]{2,1,0:T(4,128)}, f32[1,1]{1,0:T(1,128)}) custom-call(f32[209,4,128]{2,1,0:T(4,128)S(1)} %shard_map.59.result), custom_call_target="tpu_custom_call" | custom-call | tf_op jit(solution)/shard_map/pallas_call | solution.py:420

commit v6 on v5

--- a/solution.py
+++ b/solution.py
@@ -13,7 +13,7 @@
 ROWS = 4
 NEAR = 8
 PLANES = 2
-CHUNKS = ((0, 6), (6, 7))
+CHUNKS = ((0, 7), (7, 6))
 
 
 def kernel(
@@ -101,20 +101,13 @@
 
     barrier = pltpu.get_barrier_semaphore()
 
-    def greet(peer):
+    steps = sorted(range(ny), key=lambda k: -min(k, ny - k))
+    greeted = [place(y + k, z + dz) for k in steps for dz in (quarter, -quarter)]
+    greeted += [y_peer(k) for k in steps if k]
+    greeted += [z_peer(k) for k in range(1, nz) if k not in (quarter, nz - quarter)]
+    greeted += [near_peer(k) for k in range(1, NEAR)]
+    for peer in greeted:
         pl.semaphore_signal(barrier, inc=1, device_id=peer, device_id_type=MESH)
-
-    def greet_all(peer, start, count):
-        def one(k, carry):
-            greet(peer(k))
-            return carry
-
-        lax.fori_loop(start, count, one, 0)
-
-    greet_all(met, 0, members)
-    greet_all(near_peer, 1, NEAR)
-    greet_all(z_peer, 1, nz)
-    greet_all(y_peer, 1, ny)
     own_copy = pltpu.make_async_copy(ens, own, local_sem.at[0])
     tgt_copy = pltpu.make_async_copy(tgt, tgt_rows, local_sem.at[1])
     cw_copy = pltpu.make_async_copy(cw_hbm, cw, local_sem.at[2])
@@ -124,7 +117,7 @@
     own_copy.start()
     tgt_copy.start()
 
-    pl.semaphore_wait(barrier, members + (NEAR - 1) + (nz - 1) + (ny - 1))
+    pl.semaphore_wait(barrier, len(greeted))
 
     def push(src, dst, send, recv, device):
         pltpu.make_async_remote_copy(

time: 45.4 us -> 45.7 us (level)
  no operation moved by 1% of the time
where the time goes in v6:
time: 45.7 us; the launch traced here: 45.4 us
  Pallas kernels  44.8 us (98%)
  between operations  0.64 us (1%)
    pallas_call x1, Pallas kernels, local(): pl.pallas_call(body, out_shape=jax.ShapeDtypeStruct((units + 1, ROWS, BLO...  44 us

profile of v6, /device:TPU:1, one launch (start us, length us, event | category | flops | bytes accessed | tf_op | source)
XLA Modules:
  0.0 45.4 jit_solution(12699802945155296045)
XLA Ops:
  0.6 44.0 %shard_map.59.result = f32[209,4,128]{2,1,0:T(4,128)S(1)} custom-call(f32[208,4,128]{2,1,0:T(4,128)} %bitcast.4, f32[26,4096]{1,0:T(8,128)} %refs_1_.1, f32[26]{0:T(128)} %refs_2_.1, s32[1,32]{1,0:T(1,128)} %bitcast.5), custom_call_target="tpu_custom_call" | custom-call | tf_op jit(solution)/shard_map/pallas_call | solution.py:364
  44.6 0.8 %shard_map.60 = (f32[208,4,128]{2,1,0:T(4,128)}, f32[1,1]{1,0:T(1,128)}) custom-call(f32[209,4,128]{2,1,0:T(4,128)S(1)} %shard_map.59.result), custom_call_target="tpu_custom_call" | custom-call | tf_op jit(solution)/shard_map/pallas_call | solution.py:413

commit v7 on v5

--- a/solution.py
+++ b/solution.py
@@ -201,9 +201,12 @@
     tgt_copy.wait()
 
     def skill_rows(first, rows, acc):
-        for g in range(groups):
+        def group(g, acc):
             tiles = [
-                tgt_rows[pl.ds(first, rows), pl.ds((g * ROWS + i) * BLOCK, BLOCK)] for i in range(ROWS)
+                tgt_rows[
+                    pl.ds(first, rows), pl.ds(pl.multiple_of((g * ROWS + i) * BLOCK, BLOCK), BLOCK)
+                ]
+                for i in range(ROWS)
             ]
             part = jnp.zeros((ROWS, BLOCK), jnp.float32)
             for r in range(rows):
@@ -211,8 +214,9 @@
                 skill = own[u] - jnp.concatenate([tile[r : r + 1] for tile in tiles], axis=0)
                 sgn[u] = jnp.clip(skill * 64.0, -1.0, 1.0) * 0.0625
                 part = part + cw[first + r] * jnp.abs(skill)
-            acc = acc + area[g] * part
-        return acc
+            return acc + area[g] * part
+
+        return lax.fori_loop(0, groups, group, acc)
 
     def skill_octet(k, acc):
         return skill_rows(pl.multiple_of(k * 8, 8), 8, acc)
@@ -228,9 +232,11 @@
         met_area[g] = met_wide[g * ROWS : (g + 1) * ROWS]
     count = float(members)
 
-    def pairs(places, acc):
+    def pairs(k, acc):
+        last = jnp.minimum(2 * k + 1, per - 1)
+        counted = jnp.where(2 * k + 1 < per, 1.0, 0.0)
         values = [
-            jnp.concatenate([gat[j, i] for i in places], axis=0) * 64.0 for j in range(members)
+            jnp.concatenate([gat[j, 2 * k], gat[j, last]], axis=0) * 64.0 for j in range(members)
         ]
         signs = [jnp.zeros_like(values[0]) for j in range(members)]
         for a in range(members):
@@ -241,38 +247,24 @@
         dot = values[0] * signs[0]
         for j in range(1, members):
             dot = dot + values[j] * signs[j]
-        for n, i in enumerate(places):
-            part = slice(n * ROWS, (n + 1) * ROWS)
+        for i, part, factor in ((2 * k, slice(0, ROWS), 1.0), (last, slice(ROWS, 2 * ROWS), counted)):
             for j in range(members):
                 sums[j, i] = signs[j][part]
             u = m * per + i
-            acc = acc + (met_area[lax.rem(u, groups)] * cw[lax.div(u, groups)]) * dot[part]
+            acc = acc + (met_area[lax.rem(u, groups)] * (cw[lax.div(u, groups)] * factor)) * dot[part]
         return acc
 
-    spread_sum = jnp.zeros((ROWS, BLOCK), jnp.float32)
-    for chunk, (first, size) in enumerate(CHUNKS):
-
-        def wait_chunk(j, carry):
+    def wait_chunk(chunk):
+        first, size = CHUNKS[chunk]
+
+        def one(j, carry):
             arrived(gat.at[j, pl.ds(first, size)], recv1.at[chunk, j])
             return carry
 
-        lax.fori_loop(0, members, wait_chunk, 0)
-        if chunk == 0:
-            area_near = collect(box_a1, near_at, send_a1, recv_a1, NEAR)
-            box_a2[far_at] = area_near
-            share(box_a2, far_at, send_a2, recv_a2, far_peer, far)
-        spread_sum = lax.fori_loop(
-            0,
-            size // 2,
-            lambda k, acc: pairs((first + 2 * k, first + 2 * k + 1), acc),
-            spread_sum,
-        )
-        if size % 2:
-            spread_sum = pairs((first + size - 1,), spread_sum)
-        if first + size == per:
-            mine = skill_sum * (1.0 / count) - spread_sum * (1.0 / (64.0 * count * (count - 1.0)))
-            box_l1[near_at] = jnp.sum(mine, axis=0, keepdims=True)
-            share(box_l1, near_at, send_l1, recv_l1, near_peer, NEAR)
+        lax.fori_loop(0, members, one, 0)
+
+    def send_back(chunk):
+        first, size = CHUNKS[chunk]
         exchange(
             lambda j: sums.at[j, pl.ds(first, size)],
             lambda i: back.at[pl.ds(i * per + first, size)],
@@ -280,6 +272,29 @@
             recv2,
             chunk,
         )
+
+    middle = CHUNKS[1][0] // 2
+
+    def chunk_step(chunk, acc):
+        @pl.when(chunk == 0)
+        def _():
+            wait_chunk(0)
+            area_near = collect(box_a1, near_at, send_a1, recv_a1, NEAR)
+            box_a2[far_at] = area_near
+            share(box_a2, far_at, send_a2, recv_a2, far_peer, far)
+
+        @pl.when(chunk == 1)
+        def _():
+            send_back(0)
+            wait_chunk(1)
+
+        return lax.fori_loop(chunk * middle, middle + chunk * ((per + 1) // 2 - middle), pairs, acc)
+
+    spread_sum = lax.fori_loop(0, len(CHUNKS), chunk_step, jnp.zeros((ROWS, BLOCK), jnp.float32))
+    mine = skill_sum * (1.0 / count) - spread_sum * (1.0 / (64.0 * count * (count - 1.0)))
+    box_l1[near_at] = jnp.sum(mine, axis=0, keepdims=True)
+    share(box_l1, near_at, send_l1, recv_l1, near_peer, NEAR)
+    send_back(1)
 
     loss_near = collect(box_l1, near_at, send_l1, recv_l1, NEAR)
     box_l2[z] = loss_near

time: 45.4 us -> 45.4 us (level)
  no operation moved by 1% of the time
where the time goes in v7:
time: 45.4 us; the launch traced here: 45 us
  Pallas kernels  44.3 us (98%)
  between operations  0.64 us (1%)
    pallas_call x1, Pallas kernels, local(): pl.pallas_call(body, out_shape=jax.ShapeDtypeStruct((units + 1, ROWS, BLO...  43.5 us

profile of v7, /device:TPU:1, one launch (start us, length us, event | category | flops | bytes accessed | tf_op | source)
XLA Modules:
  0.0 45.0 jit_solution(15837604840899996423)
XLA Ops:
  0.6 43.5 %shard_map.59.result = f32[209,4,128]{2,1,0:T(4,128)S(1)} custom-call(f32[208,4,128]{2,1,0:T(4,128)} %bitcast.4, f32[26,4096]{1,0:T(8,128)} %refs_1_.1, f32[26]{0:T(128)} %refs_2_.1, s32[1,32]{1,0:T(1,128)} %bitcast.5), custom_call_target="tpu_custom_call" | custom-call | tf_op jit(solution)/shard_map/pallas_call | solution.py:386
  44.2 0.8 %shard_map.60 = (f32[208,4,128]{2,1,0:T(4,128)}, f32[1,1]{1,0:T(1,128)}) custom-call(f32[209,4,128]{2,1,0:T(4,128)S(1)} %shard_map.59.result), custom_call_target="tpu_custom_call" | custom-call | tf_op jit(solution)/shard_map/pallas_call | solution.py:435

commit v8 on v7

--- a/solution.py
+++ b/solution.py
@@ -292,16 +292,16 @@
 
     spread_sum = lax.fori_loop(0, len(CHUNKS), chunk_step, jnp.zeros((ROWS, BLOCK), jnp.float32))
     mine = skill_sum * (1.0 / count) - spread_sum * (1.0 / (64.0 * count * (count - 1.0)))
-    box_l1[near_at] = jnp.sum(mine, axis=0, keepdims=True)
-    share(box_l1, near_at, send_l1, recv_l1, near_peer, NEAR)
+    box_l1[z] = jnp.sum(mine, axis=0, keepdims=True)
+    share(box_l1, z, send_l1, recv_l1, z_peer, nz)
     send_back(1)
 
-    loss_near = collect(box_l1, near_at, send_l1, recv_l1, NEAR)
-    box_l2[z] = loss_near
-    share(box_l2, z, send_l2, recv_l2, z_peer, nz)
-    loss_z = collect(box_l2, z, send_l2, recv_l2, nz)
-    box_l3[y] = loss_z
-    share(box_l3, y, send_l3, recv_l3, y_peer, ny)
+    loss_z = collect(box_l1, z, send_l1, recv_l1, nz)
+    box_l2[y] = loss_z
+    share(box_l2, y, send_l2, recv_l2, y_peer, ny)
+    loss_y = collect(box_l2, y, send_l2, recv_l2, ny)
+    box_l3[near_at] = loss_y
+    share(box_l3, near_at, send_l3, recv_l3, near_peer, NEAR)
 
     area_all = collect(box_a2, far_at, send_a2, recv_a2, far)
     area_total = jnp.sum(area_all, axis=1, keepdims=True)
@@ -335,7 +335,7 @@
 
         lax.fori_loop(0, members, take_back, 0)
 
-    loss_all = collect(box_l3, y, send_l3, recv_l3, ny)
+    loss_all = collect(box_l3, near_at, send_l3, recv_l3, NEAR)
     loss_total = jnp.sum(loss_all, axis=1, keepdims=True)
     result[units] = jnp.broadcast_to(loss_total / (area_total * float(channels)), (ROWS, BLOCK))
 
@@ -403,9 +403,9 @@
             pltpu.VMEM((2, 1, lat_band.shape[0]), f32),
             box(NEAR),
             box(far),
-            box(NEAR),
             box(nz),
             box(ny),
+            box(NEAR),
             dma((4,)),
             dma((2,)),
             dma((len(CHUNKS), members)),
@@ -416,12 +416,12 @@
             dma((NEAR,)),
             dma((far,)),
             dma((far,)),
-            dma((NEAR,)),
-            dma((NEAR,)),
             dma((nz,)),
             dma((nz,)),
             dma((ny,)),
             dma((ny,)),
+            dma((NEAR,)),
+            dma((NEAR,)),
         ],
         compiler_params=pltpu.CompilerParams(
             collective_id=0, has_side_effects=True, vmem_limit_bytes=32 * 1024 * 1024

time: 45.4 us -> 48.1 us (1.059)
  Pallas kernels: 44.3 us -> 47.3 us
    pallas_call x1, Pallas kernels: 43.5 us -> 46.5 us  [local(): pl.pallas_call(body, out_shape=jax.ShapeDtypeStruct((units + 1, ROWS, BLO...]
where the time goes in v8:
time: 48.1 us; the launch traced here: 48 us
  Pallas kernels  47.3 us (98%)
  between operations  0.64 us (1%)
    pallas_call x1, Pallas kernels, local(): pl.pallas_call(body, out_shape=jax.ShapeDtypeStruct((units + 1, ROWS, BLO...  46.5 us

profile of v8, /device:TPU:1, one launch (start us, length us, event | category | flops | bytes accessed | tf_op | source)
XLA Modules:
  0.0 48.0 jit_solution(16235471443656747836)
XLA Ops:
  0.6 46.5 %shard_map.59.result = f32[209,4,128]{2,1,0:T(4,128)S(1)} custom-call(f32[208,4,128]{2,1,0:T(4,128)} %bitcast.4, f32[26,4096]{1,0:T(8,128)} %refs_1_.1, f32[26]{0:T(128)} %refs_2_.1, s32[1,32]{1,0:T(1,128)} %bitcast.5), custom_call_target="tpu_custom_call" | custom-call | tf_op jit(solution)/shard_map/pallas_call | solution.py:386
  47.2 0.8 %shard_map.60 = (f32[208,4,128]{2,1,0:T(4,128)}, f32[1,1]{1,0:T(1,128)}) custom-call(f32[209,4,128]{2,1,0:T(4,128)S(1)} %shard_map.59.result), custom_call_target="tpu_custom_call" | custom-call | tf_op jit(solution)/shard_map/pallas_call | solution.py:435

commit v9 on v7

--- a/solution.py
+++ b/solution.py
@@ -136,14 +136,14 @@
             device_id_type=MESH,
         ).start()
 
-    def exchange(source, landing, send, recv, chunk):
+    def exchange(source, landing, send, recv, chunk, start, stop):
         def one(n, carry):
             device = met(n)
             j = device[0]
             push(source(j), landing(m), send.at[chunk, j], recv.at[chunk, m], device)
             return carry
 
-        lax.fori_loop(0, members, one, 0)
+        lax.fori_loop(start, stop, one, 0)
 
     def arrived(ref, sem):
         pltpu.make_async_copy(ref, ref, sem).wait()
@@ -175,6 +175,8 @@
             send1,
             recv1,
             chunk,
+            0,
+            members,
         )
 
     def along_rows(row):
@@ -263,7 +265,7 @@
 
         lax.fori_loop(0, members, one, 0)
 
-    def send_back(chunk):
+    def send_back(chunk, start, stop):
         first, size = CHUNKS[chunk]
         exchange(
             lambda j: sums.at[j, pl.ds(first, size)],
@@ -271,6 +273,8 @@
             send2,
             recv2,
             chunk,
+            start,
+            stop,
         )
 
     middle = CHUNKS[1][0] // 2
@@ -285,7 +289,7 @@
 
         @pl.when(chunk == 1)
         def _():
-            send_back(0)
+            send_back(0, 0, members)
             wait_chunk(1)
 
         return lax.fori_loop(chunk * middle, middle + chunk * ((per + 1) // 2 - middle), pairs, acc)
@@ -294,11 +298,11 @@
     mine = skill_sum * (1.0 / count) - spread_sum * (1.0 / (64.0 * count * (count - 1.0)))
     box_l1[near_at] = jnp.sum(mine, axis=0, keepdims=True)
     share(box_l1, near_at, send_l1, recv_l1, near_peer, NEAR)
-    send_back(1)
-
+    send_back(1, 0, members // 2)
     loss_near = collect(box_l1, near_at, send_l1, recv_l1, NEAR)
     box_l2[z] = loss_near
     share(box_l2, z, send_l2, recv_l2, z_peer, nz)
+    send_back(1, members // 2, members)
     loss_z = collect(box_l2, z, send_l2, recv_l2, nz)
     box_l3[y] = loss_z
     share(box_l3, y, send_l3, recv_l3, y_peer, ny)

time: 45.4 us -> 46 us (1.013)
  Pallas kernels: 44.3 us -> 45.2 us
    pallas_call x1, Pallas kernels: 43.5 us -> 44.4 us  [local(): pl.pallas_call(body, out_shape=jax.ShapeDtypeStruct((units + 1, ROWS, BLO...]
where the time goes in v9:
time: 46 us; the launch traced here: 45.8 us
  Pallas kernels  45.2 us (98%)
  between operations  0.64 us (1%)
    pallas_call x1, Pallas kernels, local(): pl.pallas_call(body, out_shape=jax.ShapeDtypeStruct((units + 1, ROWS, BLO...  44.4 us

profile of v9, /device:TPU:1, one launch (start us, length us, event | category | flops | bytes accessed | tf_op | source)
XLA Modules:
  0.0 45.8 jit_solution(4305898828860614011)
XLA Ops:
  0.6 44.4 %shard_map.59.result = f32[209,4,128]{2,1,0:T(4,128)S(1)} custom-call(f32[208,4,128]{2,1,0:T(4,128)} %bitcast.4, f32[26,4096]{1,0:T(8,128)} %refs_1_.1, f32[26]{0:T(128)} %refs_2_.1, s32[1,32]{1,0:T(1,128)} %bitcast.5), custom_call_target="tpu_custom_call" | custom-call | tf_op jit(solution)/shard_map/pallas_call | solution.py:390
  45.1 0.8 %shard_map.60 = (f32[208,4,128]{2,1,0:T(4,128)}, f32[1,1]{1,0:T(1,128)}) custom-call(f32[209,4,128]{2,1,0:T(4,128)S(1)} %shard_map.59.result), custom_call_target="tpu_custom_call" | custom-call | tf_op jit(solution)/shard_map/pallas_call | solution.py:439

commit v10 on v7

--- a/solution.py
+++ b/solution.py
@@ -101,6 +101,9 @@
 
     barrier = pltpu.get_barrier_semaphore()
 
+    own_copy = pltpu.make_async_copy(ens, own, local_sem.at[0])
+    own_copy.start()
+
     def greet(peer):
         pl.semaphore_signal(barrier, inc=1, device_id=peer, device_id_type=MESH)
 
@@ -115,13 +118,11 @@
     greet_all(near_peer, 1, NEAR)
     greet_all(z_peer, 1, nz)
     greet_all(y_peer, 1, ny)
-    own_copy = pltpu.make_async_copy(ens, own, local_sem.at[0])
     tgt_copy = pltpu.make_async_copy(tgt, tgt_rows, local_sem.at[1])
     cw_copy = pltpu.make_async_copy(cw_hbm, cw, local_sem.at[2])
     lat_copy = pltpu.make_async_copy(lat_hbm, lat, local_sem.at[3])
     lat_copy.start()
     cw_copy.start()
-    own_copy.start()
     tgt_copy.start()
 
     pl.semaphore_wait(barrier, members + (NEAR - 1) + (nz - 1) + (ny - 1))
@@ -168,9 +169,10 @@
             total = total + box[j]
         return total
 
+    own_copy.wait()
     for chunk, (first, size) in enumerate(CHUNKS):
         exchange(
-            lambda j: ens.at[pl.ds(j * per + first, size)],
+            lambda j: own.at[pl.ds(j * per + first, size)],
             lambda i: gat.at[i, pl.ds(first, size)],
             send1,
             recv1,
@@ -197,7 +199,6 @@
     share(box_a1, near_at, send_a1, recv_a1, near_peer, NEAR)
 
     cw_copy.wait()
-    own_copy.wait()
     tgt_copy.wait()
 
     def skill_rows(first, rows, acc):

time: 45.4 us -> 45.2 us (level)
  no operation moved by 1% of the time
where the time goes in v10:
time: 45.2 us; the launch traced here: 44.8 us
  Pallas kernels  44.1 us (98%)
  between operations  0.64 us (1%)
    pallas_call x1, Pallas kernels, local(): pl.pallas_call(body, out_shape=jax.ShapeDtypeStruct((units + 1, ROWS, BLO...  43.3 us

profile of v10, /device:TPU:1, one launch (start us, length us, event | category | flops | bytes accessed | tf_op | source)
XLA Modules:
  0.0 44.8 jit_solution(199032841804999829)
XLA Ops:
  0.6 43.3 %shard_map.59.result = f32[209,4,128]{2,1,0:T(4,128)S(1)} custom-call(f32[208,4,128]{2,1,0:T(4,128)} %bitcast.4, f32[26,4096]{1,0:T(8,128)} %refs_1_.1, f32[26]{0:T(128)} %refs_2_.1, s32[1,32]{1,0:T(1,128)} %bitcast.5), custom_call_target="tpu_custom_call" | custom-call | tf_op jit(solution)/shard_map/pallas_call | solution.py:387
  44.0 0.8 %shard_map.60 = (f32[208,4,128]{2,1,0:T(4,128)}, f32[1,1]{1,0:T(1,128)}) custom-call(f32[209,4,128]{2,1,0:T(4,128)S(1)} %shard_map.59.result), custom_call_target="tpu_custom_call" | custom-call | tf_op jit(solution)/shard_map/pallas_call | solution.py:436

commit v11 on v7

--- a/solution.py
+++ b/solution.py
@@ -13,7 +13,7 @@
 ROWS = 4
 NEAR = 8
 PLANES = 2
-CHUNKS = ((0, 6), (6, 7))
+CHUNKS = ((0, 8), (8, 5))
 
 
 def kernel(

time: 45.4 us -> 46.7 us (1.029)
  Pallas kernels: 44.3 us -> 45.6 us
    pallas_call x1, Pallas kernels: 43.5 us -> 44.8 us  [local(): pl.pallas_call(body, out_shape=jax.ShapeDtypeStruct((units + 1, ROWS, BLO...]
where the time goes in v11:
time: 46.7 us; the launch traced here: 46.2 us
  Pallas kernels  45.6 us (98%)
  between operations  0.64 us (1%)
    pallas_call x1, Pallas kernels, local(): pl.pallas_call(body, out_shape=jax.ShapeDtypeStruct((units + 1, ROWS, BLO...  44.8 us

profile of v11, /device:TPU:1, one launch (start us, length us, event | category | flops | bytes accessed | tf_op | source)
XLA Modules:
  0.0 46.2 jit_solution(3766524307841436615)
XLA Ops:
  0.6 44.8 %shard_map.59.result = f32[209,4,128]{2,1,0:T(4,128)S(1)} custom-call(f32[208,4,128]{2,1,0:T(4,128)} %bitcast.4, f32[26,4096]{1,0:T(8,128)} %refs_1_.1, f32[26]{0:T(128)} %refs_2_.1, s32[1,32]{1,0:T(1,128)} %bitcast.5), custom_call_target="tpu_custom_call" | custom-call | tf_op jit(solution)/shard_map/pallas_call | solution.py:386
  45.5 0.8 %shard_map.60 = (f32[208,4,128]{2,1,0:T(4,128)}, f32[1,1]{1,0:T(1,128)}) custom-call(f32[209,4,128]{2,1,0:T(4,128)S(1)} %shard_map.59.result), custom_call_target="tpu_custom_call" | custom-call | tf_op jit(solution)/shard_map/pallas_call | solution.py:435

commit v12 on v11

--- a/solution.py
+++ b/solution.py
@@ -13,7 +13,7 @@
 ROWS = 4
 NEAR = 8
 PLANES = 2
-CHUNKS = ((0, 8), (8, 5))
+CHUNKS = ((0, 4), (4, 9))
 
 
 def kernel(

time: 46.7 us -> 47 us (level)
  no operation moved by 1% of the time
where the time goes in v12:
time: 47 us; the launch traced here: 46.5 us
  Pallas kernels  45.9 us (98%)
  between operations  0.64 us (1%)
    pallas_call x1, Pallas kernels, local(): pl.pallas_call(body, out_shape=jax.ShapeDtypeStruct((units + 1, ROWS, BLO...  45.1 us

profile of v12, /device:TPU:1, one launch (start us, length us, event | category | flops | bytes accessed | tf_op | source)
XLA Modules:
  0.0 46.5 jit_solution(12946536056207822778)
XLA Ops:
  0.6 45.1 %shard_map.59.result = f32[209,4,128]{2,1,0:T(4,128)S(1)} custom-call(f32[208,4,128]{2,1,0:T(4,128)} %bitcast.4, f32[26,4096]{1,0:T(8,128)} %refs_1_.1, f32[26]{0:T(128)} %refs_2_.1, s32[1,32]{1,0:T(1,128)} %bitcast.5), custom_call_target="tpu_custom_call" | custom-call | tf_op jit(solution)/shard_map/pallas_call | solution.py:386
  45.8 0.8 %shard_map.60 = (f32[208,4,128]{2,1,0:T(4,128)}, f32[1,1]{1,0:T(1,128)}) custom-call(f32[209,4,128]{2,1,0:T(4,128)S(1)} %shard_map.59.result), custom_call_target="tpu_custom_call" | custom-call | tf_op jit(solution)/shard_map/pallas_call | solution.py:435

commit v13 on v7

--- a/solution.py
+++ b/solution.py
@@ -155,11 +155,17 @@
 
         lax.fori_loop(1, count, one, 0)
 
-    def collect(box, at, send, recv, count):
+    def sent(box, send, count):
+        def one(k, carry):
+            arrived(box.at[0], send.at[k])
+            return carry
+
+        lax.fori_loop(1, count, one, 0)
+
+    def collect(box, at, recv, count):
         def one(k, carry):
             j = lax.rem(at + k, count)
-            pltpu.make_async_copy(box.at[j], box.at[j], recv.at[j]).wait()
-            pltpu.make_async_copy(box.at[at], box.at[at], send.at[k]).wait()
+            arrived(box.at[j], recv.at[j])
             return carry
 
         lax.fori_loop(1, count, one, 0)
@@ -279,7 +285,7 @@
         @pl.when(chunk == 0)
         def _():
             wait_chunk(0)
-            area_near = collect(box_a1, near_at, send_a1, recv_a1, NEAR)
+            area_near = collect(box_a1, near_at, recv_a1, NEAR)
             box_a2[far_at] = area_near
             share(box_a2, far_at, send_a2, recv_a2, far_peer, far)
 
@@ -296,14 +302,14 @@
     share(box_l1, near_at, send_l1, recv_l1, near_peer, NEAR)
     send_back(1)
 
-    loss_near = collect(box_l1, near_at, send_l1, recv_l1, NEAR)
+    loss_near = collect(box_l1, near_at, recv_l1, NEAR)
     box_l2[z] = loss_near
     share(box_l2, z, send_l2, recv_l2, z_peer, nz)
-    loss_z = collect(box_l2, z, send_l2, recv_l2, nz)
+    loss_z = collect(box_l2, z, recv_l2, nz)
     box_l3[y] = loss_z
     share(box_l3, y, send_l3, recv_l3, y_peer, ny)
 
-    area_all = collect(box_a2, far_at, send_a2, recv_a2, far)
+    area_all = collect(box_a2, far_at, recv_a2, far)
     area_total = jnp.sum(area_all, axis=1, keepdims=True)
     points = float(units * ROWS * BLOCK // channels * spaces)
     factor = jnp.broadcast_to(points / area_total, (ROWS, BLOCK))
@@ -335,7 +341,7 @@
 
         lax.fori_loop(0, members, take_back, 0)
 
-    loss_all = collect(box_l3, y, send_l3, recv_l3, ny)
+    loss_all = collect(box_l3, y, recv_l3, ny)
     loss_total = jnp.sum(loss_all, axis=1, keepdims=True)
     result[units] = jnp.broadcast_to(loss_total / (area_total * float(channels)), (ROWS, BLOCK))
 
@@ -348,6 +354,11 @@
 
         lax.fori_loop(0, members, wait_sent, 0)
     arrived(box_row.at[0], row_sem.at[0])
+    sent(box_a1, send_a1, NEAR)
+    sent(box_a2, send_a2, far)
+    sent(box_l1, send_l1, NEAR)
+    sent(box_l2, send_l2, nz)
+    sent(box_l3, send_l3, ny)
 
 
 def deliver(result, grad, loss, last, sem):

time: 45.4 us -> 45.6 us (level)
  no operation moved by 1% of the time
where the time goes in v13:
time: 45.6 us; the launch traced here: 45.1 us
  Pallas kernels  44.5 us (98%)
  between operations  0.64 us (1%)
    pallas_call x1, Pallas kernels, local(): pl.pallas_call(body, out_shape=jax.ShapeDtypeStruct((units + 1, ROWS, BLO...  43.7 us

profile of v13, /device:TPU:1, one launch (start us, length us, event | category | flops | bytes accessed | tf_op | source)
XLA Modules:
  0.0 45.1 jit_solution(10021502150342701481)
XLA Ops:
  0.6 43.7 %shard_map.59.result = f32[209,4,128]{2,1,0:T(4,128)S(1)} custom-call(f32[208,4,128]{2,1,0:T(4,128)} %bitcast.4, f32[26,4096]{1,0:T(8,128)} %refs_1_.1, f32[26]{0:T(128)} %refs_2_.1, s32[1,32]{1,0:T(1,128)} %bitcast.5), custom_call_target="tpu_custom_call" | custom-call | tf_op jit(solution)/shard_map/pallas_call | solution.py:397
  44.4 0.8 %shard_map.60 = (f32[208,4,128]{2,1,0:T(4,128)}, f32[1,1]{1,0:T(1,128)}) custom-call(f32[209,4,128]{2,1,0:T(4,128)S(1)} %shard_map.59.result), custom_call_target="tpu_custom_call" | custom-call | tf_op jit(solution)/shard_map/pallas_call | solution.py:446

commit v14 on v13

--- a/solution.py
+++ b/solution.py
@@ -285,22 +285,22 @@
         @pl.when(chunk == 0)
         def _():
             wait_chunk(0)
+
+        @pl.when(chunk == 1)
+        def _():
+            send_back(0)
             area_near = collect(box_a1, near_at, recv_a1, NEAR)
             box_a2[far_at] = area_near
             share(box_a2, far_at, send_a2, recv_a2, far_peer, far)
-
-        @pl.when(chunk == 1)
-        def _():
-            send_back(0)
             wait_chunk(1)
 
         return lax.fori_loop(chunk * middle, middle + chunk * ((per + 1) // 2 - middle), pairs, acc)
 
     spread_sum = lax.fori_loop(0, len(CHUNKS), chunk_step, jnp.zeros((ROWS, BLOCK), jnp.float32))
+    send_back(1)
     mine = skill_sum * (1.0 / count) - spread_sum * (1.0 / (64.0 * count * (count - 1.0)))
     box_l1[near_at] = jnp.sum(mine, axis=0, keepdims=True)
     share(box_l1, near_at, send_l1, recv_l1, near_peer, NEAR)
-    send_back(1)
 
     loss_near = collect(box_l1, near_at, recv_l1, NEAR)
     box_l2[z] = loss_near

time: 45.6 us -> 45.9 us (level)
  Pallas kernels: 44.5 us -> 45.1 us
    pallas_call x1, Pallas kernels: 43.7 us -> 44.4 us  [local(): pl.pallas_call(body, out_shape=jax.ShapeDtypeStruct((units + 1, ROWS, BLO...]
where the time goes in v14:
time: 45.9 us; the launch traced here: 45.8 us
  Pallas kernels  45.1 us (98%)
  between operations  0.64 us (1%)
    pallas_call x1, Pallas kernels, local(): pl.pallas_call(body, out_shape=jax.ShapeDtypeStruct((units + 1, ROWS, BLO...  44.4 us

profile of v14, /device:TPU:1, one launch (start us, length us, event | category | flops | bytes accessed | tf_op | source)
XLA Modules:
  0.0 45.8 jit_solution(17077591204204112026)
XLA Ops:
  0.6 44.4 %shard_map.59.result = f32[209,4,128]{2,1,0:T(4,128)S(1)} custom-call(f32[208,4,128]{2,1,0:T(4,128)} %bitcast.4, f32[26,4096]{1,0:T(8,128)} %refs_1_.1, f32[26]{0:T(128)} %refs_2_.1, s32[1,32]{1,0:T(1,128)} %bitcast.5), custom_call_target="tpu_custom_call" | custom-call | tf_op jit(solution)/shard_map/pallas_call | solution.py:397
  45.0 0.8 %shard_map.60 = (f32[208,4,128]{2,1,0:T(4,128)}, f32[1,1]{1,0:T(1,128)}) custom-call(f32[209,4,128]{2,1,0:T(4,128)S(1)} %shard_map.59.result), custom_call_target="tpu_custom_call" | custom-call | tf_op jit(solution)/shard_map/pallas_call | solution.py:446

commit v15 on v7

--- a/solution.py
+++ b/solution.py
@@ -93,11 +93,13 @@
 
     quarter = nz // 4
 
+    mirror = 1 - 2 * lax.rem(s, 2)
+
     def met(n):
         pair, turn = lax.div(n, 4), lax.rem(n, 4)
         dy = ny // 2 - pair + lax.rem(turn, 2) * (2 * pair - ny + 1)
         dz = quarter * (1 - 2 * lax.rem(lax.div(turn + 1, 2), 2))
-        return place(y + dy, z + dz)
+        return place(y + mirror * dy, z + mirror * dz)
 
     barrier = pltpu.get_barrier_semaphore()
 

time: 45.4 us -> 45.4 us (level)
  no operation moved by 1% of the time
where the time goes in v15:
time: 45.4 us; the launch traced here: 45.3 us
  Pallas kernels  44.7 us (98%)
  between operations  0.64 us (1%)
    pallas_call x1, Pallas kernels, local(): pl.pallas_call(body, out_shape=jax.ShapeDtypeStruct((units + 1, ROWS, BLO...  43.9 us

profile of v15, /device:TPU:1, one launch (start us, length us, event | category | flops | bytes accessed | tf_op | source)
XLA Modules:
  0.0 45.3 jit_solution(12939535842960229856)
XLA Ops:
  0.6 43.9 %shard_map.59.result = f32[209,4,128]{2,1,0:T(4,128)S(1)} custom-call(f32[208,4,128]{2,1,0:T(4,128)} %bitcast.4, f32[26,4096]{1,0:T(8,128)} %refs_1_.1, f32[26]{0:T(128)} %refs_2_.1, s32[1,32]{1,0:T(1,128)} %bitcast.5), custom_call_target="tpu_custom_call" | custom-call | tf_op jit(solution)/shard_map/pallas_call | solution.py:388
  44.5 0.8 %shard_map.60 = (f32[208,4,128]{2,1,0:T(4,128)}, f32[1,1]{1,0:T(1,128)}) custom-call(f32[209,4,128]{2,1,0:T(4,128)S(1)} %shard_map.59.result), custom_call_target="tpu_custom_call" | custom-call | tf_op jit(solution)/shard_map/pallas_call | solution.py:437

commit v16 on v7

--- a/solution.py
+++ b/solution.py
@@ -93,11 +93,17 @@
 
     quarter = nz // 4
 
-    def met(n):
-        pair, turn = lax.div(n, 4), lax.rem(n, 4)
-        dy = ny // 2 - pair + lax.rem(turn, 2) * (2 * pair - ny + 1)
-        dz = quarter * (1 - 2 * lax.rem(lax.div(turn + 1, 2), 2))
-        return place(y + dy, z + dz)
+    up, down = place(0, z + quarter), place(0, z - quarter)
+
+    def each_met(visit):
+        def four(pair, carry):
+            ahead = lax.rem(y + (ny + ny // 2) - pair, ny) * PLANES
+            behind = lax.rem(y + (ny // 2 + 1) + pair, ny) * PLANES
+            for along, plane in ((ahead, up), (behind, down), (ahead, down), (behind, up)):
+                visit((along + plane[0], plane[1]))
+            return carry
+
+        lax.fori_loop(0, ny // 2, four, 0)
 
     barrier = pltpu.get_barrier_semaphore()
 
@@ -111,7 +117,7 @@
 
         lax.fori_loop(start, count, one, 0)
 
-    greet_all(met, 0, members)
+    each_met(greet)
     greet_all(near_peer, 1, NEAR)
     greet_all(z_peer, 1, nz)
     greet_all(y_peer, 1, ny)
@@ -137,13 +143,11 @@
         ).start()
 
     def exchange(source, landing, send, recv, chunk):
-        def one(n, carry):
-            device = met(n)
+        def one(device):
             j = device[0]
             push(source(j), landing(m), send.at[chunk, j], recv.at[chunk, m], device)
-            return carry
-
-        lax.fori_loop(0, members, one, 0)
+
+        each_met(one)
 
     def arrived(ref, sem):
         pltpu.make_async_copy(ref, ref, sem).wait()
@@ -326,8 +330,7 @@
 
     for chunk, (first, size) in enumerate(CHUNKS):
 
-        def take_back(n, carry):
-            j = met(n)[0]
+        def take_back(j, carry):
             part = back.at[pl.ds(j * per + first, size)]
             arrived(part, recv2.at[chunk, j])
             finish(j, part[...], first, size)

time: 45.4 us -> 45.2 us (level)
  no operation moved by 1% of the time
where the time goes in v16:
time: 45.2 us; the launch traced here: 45.1 us
  Pallas kernels  44.5 us (98%)
  between operations  0.64 us (1%)
    pallas_call x1, Pallas kernels, local(): pl.pallas_call(body, out_shape=jax.ShapeDtypeStruct((units + 1, ROWS, BLO...  43.7 us

profile of v16, /device:TPU:1, one launch (start us, length us, event | category | flops | bytes accessed | tf_op | source)
XLA Modules:
  0.0 45.1 jit_solution(9491970188700721331)
XLA Ops:
  0.6 43.7 %shard_map.59.result = f32[209,4,128]{2,1,0:T(4,128)S(1)} custom-call(f32[208,4,128]{2,1,0:T(4,128)} %bitcast.4, f32[26,4096]{1,0:T(8,128)} %refs_1_.1, f32[26]{0:T(128)} %refs_2_.1, s32[1,32]{1,0:T(1,128)} %bitcast.5), custom_call_target="tpu_custom_call" | custom-call | tf_op jit(solution)/shard_map/pallas_call | solution.py:389
  44.3 0.8 %shard_map.60 = (f32[208,4,128]{2,1,0:T(4,128)}, f32[1,1]{1,0:T(1,128)}) custom-call(f32[209,4,128]{2,1,0:T(4,128)S(1)} %shard_map.59.result), custom_call_target="tpu_custom_call" | custom-call | tf_op jit(solution)/shard_map/pallas_call | solution.py:438

commit v17 on v16

--- a/solution.py
+++ b/solution.py
@@ -86,10 +86,11 @@
         return (m, lax.rem(far_at + k, far) * NEAR + near_at)
 
     def z_peer(k):
-        return place(y, z + k)
+        zz = lax.rem(z + k, nz)
+        return (y * PLANES + lax.div(zz, far), lax.rem(zz, far) * NEAR + near_at)
 
     def y_peer(k):
-        return place(y + k, z)
+        return (lax.rem(m + k * PLANES, members), s)
 
     quarter = nz // 4
 
@@ -283,13 +284,13 @@
         @pl.when(chunk == 0)
         def _():
             wait_chunk(0)
+
+        @pl.when(chunk == 1)
+        def _():
+            send_back(0)
             area_near = collect(box_a1, near_at, send_a1, recv_a1, NEAR)
             box_a2[far_at] = area_near
             share(box_a2, far_at, send_a2, recv_a2, far_peer, far)
-
-        @pl.when(chunk == 1)
-        def _():
-            send_back(0)
             wait_chunk(1)
 
         return lax.fori_loop(chunk * middle, middle + chunk * ((per + 1) // 2 - middle), pairs, acc)

time: 45.2 us -> 45.2 us (level)
  no operation moved by 1% of the time
where the time goes in v17:
time: 45.2 us; the launch traced here: 45.1 us
  Pallas kernels  44.5 us (98%)
  between operations  0.64 us (1%)
    pallas_call x1, Pallas kernels, local(): pl.pallas_call(body, out_shape=jax.ShapeDtypeStruct((units + 1, ROWS, BLO...  43.7 us

profile of v17, /device:TPU:1, one launch (start us, length us, event | category | flops | bytes accessed | tf_op | source)
XLA Modules:
  0.0 45.1 jit_solution(14023519550054438306)
XLA Ops:
  0.6 43.7 %shard_map.59.result = f32[209,4,128]{2,1,0:T(4,128)S(1)} custom-call(f32[208,4,128]{2,1,0:T(4,128)} %bitcast.4, f32[26,4096]{1,0:T(8,128)} %refs_1_.1, f32[26]{0:T(128)} %refs_2_.1, s32[1,32]{1,0:T(1,128)} %bitcast.5), custom_call_target="tpu_custom_call" | custom-call | tf_op jit(solution)/shard_map/pallas_call | solution.py:390
  44.3 0.8 %shard_map.60 = (f32[208,4,128]{2,1,0:T(4,128)}, f32[1,1]{1,0:T(1,128)}) custom-call(f32[209,4,128]{2,1,0:T(4,128)S(1)} %shard_map.59.result), custom_call_target="tpu_custom_call" | custom-call | tf_op jit(solution)/shard_map/pallas_call | solution.py:439

commit v18 on v16

--- a/solution.py
+++ b/solution.py
@@ -95,7 +95,7 @@
 
     up, down = place(0, z + quarter), place(0, z - quarter)
 
-    def each_met(visit):
+    def each_met(visit, start=0, stop=ny // 2):
         def four(pair, carry):
             ahead = lax.rem(y + (ny + ny // 2) - pair, ny) * PLANES
             behind = lax.rem(y + (ny // 2 + 1) + pair, ny) * PLANES
@@ -103,7 +103,7 @@
                 visit((along + plane[0], plane[1]))
             return carry
 
-        lax.fori_loop(0, ny // 2, four, 0)
+        lax.fori_loop(start, stop, four, 0)
 
     barrier = pltpu.get_barrier_semaphore()
 
@@ -142,12 +142,12 @@
             device_id_type=MESH,
         ).start()
 
-    def exchange(source, landing, send, recv, chunk):
+    def exchange(source, landing, send, recv, chunk, *span):
         def one(device):
             j = device[0]
             push(source(j), landing(m), send.at[chunk, j], recv.at[chunk, m], device)
 
-        each_met(one)
+        each_met(one, *span)
 
     def arrived(ref, sem):
         pltpu.make_async_copy(ref, ref, sem).wait()
@@ -267,7 +267,7 @@
 
         lax.fori_loop(0, members, one, 0)
 
-    def send_back(chunk):
+    def send_back(chunk, *span):
         first, size = CHUNKS[chunk]
         exchange(
             lambda j: sums.at[j, pl.ds(first, size)],
@@ -275,6 +275,7 @@
             send2,
             recv2,
             chunk,
+            *span,
         )
 
     middle = CHUNKS[1][0] // 2
@@ -295,10 +296,11 @@
         return lax.fori_loop(chunk * middle, middle + chunk * ((per + 1) // 2 - middle), pairs, acc)
 
     spread_sum = lax.fori_loop(0, len(CHUNKS), chunk_step, jnp.zeros((ROWS, BLOCK), jnp.float32))
+    send_back(1, 0, ny // 4)
     mine = skill_sum * (1.0 / count) - spread_sum * (1.0 / (64.0 * count * (count - 1.0)))
     box_l1[near_at] = jnp.sum(mine, axis=0, keepdims=True)
     share(box_l1, near_at, send_l1, recv_l1, near_peer, NEAR)
-    send_back(1)
+    send_back(1, ny // 4, ny // 2)
 
     loss_near = collect(box_l1, near_at, send_l1, recv_l1, NEAR)
     box_l2[z] = loss_near

time: 45.2 us -> 45.1 us (level)
  no operation moved by 1% of the time
where the time goes in v18:
time: 45.1 us; the launch traced here: 45 us
  Pallas kernels  44.4 us (98%)
  between operations  0.64 us (1%)
    pallas_call x1, Pallas kernels, local(): pl.pallas_call(body, out_shape=jax.ShapeDtypeStruct((units + 1, ROWS, BLO...  43.6 us

profile of v18, /device:TPU:1, one launch (start us, length us, event | category | flops | bytes accessed | tf_op | source)
XLA Modules:
  0.0 45.0 jit_solution(3526615403086980385)
XLA Ops:
  0.6 43.6 %shard_map.59.result = f32[209,4,128]{2,1,0:T(4,128)S(1)} custom-call(f32[208,4,128]{2,1,0:T(4,128)} %bitcast.4, f32[26,4096]{1,0:T(8,128)} %refs_1_.1, f32[26]{0:T(128)} %refs_2_.1, s32[1,32]{1,0:T(1,128)} %bitcast.5), custom_call_target="tpu_custom_call" | custom-call | tf_op jit(solution)/shard_map/pallas_call | solution.py:391
  44.2 0.8 %shard_map.60 = (f32[208,4,128]{2,1,0:T(4,128)}, f32[1,1]{1,0:T(1,128)}) custom-call(f32[209,4,128]{2,1,0:T(4,128)S(1)} %shard_map.59.result), custom_call_target="tpu_custom_call" | custom-call | tf_op jit(solution)/shard_map/pallas_call | solution.py:440

commit v19 on v18

--- a/solution.py
+++ b/solution.py
@@ -159,11 +159,17 @@
 
         lax.fori_loop(1, count, one, 0)
 
-    def collect(box, at, send, recv, count):
+    def sent(box, send, count):
+        def one(k, carry):
+            arrived(box.at[0], send.at[k])
+            return carry
+
+        lax.fori_loop(1, count, one, 0)
+
+    def collect(box, at, recv, count):
         def one(k, carry):
             j = lax.rem(at + k, count)
-            pltpu.make_async_copy(box.at[j], box.at[j], recv.at[j]).wait()
-            pltpu.make_async_copy(box.at[at], box.at[at], send.at[k]).wait()
+            arrived(box.at[j], recv.at[j])
             return carry
 
         lax.fori_loop(1, count, one, 0)
@@ -284,7 +290,7 @@
         @pl.when(chunk == 0)
         def _():
             wait_chunk(0)
-            area_near = collect(box_a1, near_at, send_a1, recv_a1, NEAR)
+            area_near = collect(box_a1, near_at, recv_a1, NEAR)
             box_a2[far_at] = area_near
             share(box_a2, far_at, send_a2, recv_a2, far_peer, far)
 
@@ -302,14 +308,14 @@
     share(box_l1, near_at, send_l1, recv_l1, near_peer, NEAR)
     send_back(1, ny // 4, ny // 2)
 
-    loss_near = collect(box_l1, near_at, send_l1, recv_l1, NEAR)
+    loss_near = collect(box_l1, near_at, recv_l1, NEAR)
     box_l2[z] = loss_near
     share(box_l2, z, send_l2, recv_l2, z_peer, nz)
-    loss_z = collect(box_l2, z, send_l2, recv_l2, nz)
+    loss_z = collect(box_l2, z, recv_l2, nz)
     box_l3[y] = loss_z
     share(box_l3, y, send_l3, recv_l3, y_peer, ny)
 
-    area_all = collect(box_a2, far_at, send_a2, recv_a2, far)
+    area_all = collect(box_a2, far_at, recv_a2, far)
     area_total = jnp.sum(area_all, axis=1, keepdims=True)
     points = float(units * ROWS * BLOCK // channels * spaces)
     factor = jnp.broadcast_to(points / area_total, (ROWS, BLOCK))
@@ -340,7 +346,7 @@
 
         lax.fori_loop(0, members, take_back, 0)
 
-    loss_all = collect(box_l3, y, send_l3, recv_l3, ny)
+    loss_all = collect(box_l3, y, recv_l3, ny)
     loss_total = jnp.sum(loss_all, axis=1, keepdims=True)
     result[units] = jnp.broadcast_to(loss_total / (area_total * float(channels)), (ROWS, BLOCK))
 
@@ -353,6 +359,11 @@
 
         lax.fori_loop(0, members, wait_sent, 0)
     arrived(box_row.at[0], row_sem.at[0])
+    sent(box_a1, send_a1, NEAR)
+    sent(box_a2, send_a2, far)
+    sent(box_l1, send_l1, NEAR)
+    sent(box_l2, send_l2, nz)
+    sent(box_l3, send_l3, ny)
 
 
 def deliver(result, grad, loss, last, sem):

time: 45.1 us -> 45.3 us (level)
  no operation moved by 1% of the time
where the time goes in v19:
time: 45.3 us; the launch traced here: 45.1 us
  Pallas kernels  44.5 us (98%)
  between operations  0.64 us (1%)
    pallas_call x1, Pallas kernels, local(): pl.pallas_call(body, out_shape=jax.ShapeDtypeStruct((units + 1, ROWS, BLO...  43.7 us

profile of v19, /device:TPU:1, one launch (start us, length us, event | category | flops | bytes accessed | tf_op | source)
XLA Modules:
  0.0 45.1 jit_solution(224709225605546737)
XLA Ops:
  0.6 43.7 %shard_map.59.result = f32[209,4,128]{2,1,0:T(4,128)S(1)} custom-call(f32[208,4,128]{2,1,0:T(4,128)} %bitcast.4, f32[26,4096]{1,0:T(8,128)} %refs_1_.1, f32[26]{0:T(128)} %refs_2_.1, s32[1,32]{1,0:T(1,128)} %bitcast.5), custom_call_target="tpu_custom_call" | custom-call | tf_op jit(solution)/shard_map/pallas_call | solution.py:402
  44.4 0.8 %shard_map.60 = (f32[208,4,128]{2,1,0:T(4,128)}, f32[1,1]{1,0:T(1,128)}) custom-call(f32[209,4,128]{2,1,0:T(4,128)S(1)} %shard_map.59.result), custom_call_target="tpu_custom_call" | custom-call | tf_op jit(solution)/shard_map/pallas_call | solution.py:451
